TPU v7x, 32 devices: a whole 2x2x4 slice. The times are simulated.
32 devices in a mesh: chain: 2 (over x), ang: 4 (over y, core), dist: 4 (over z).
Axes of the slice: x: 2, y: 2, z: 4, core: 2. Of those that a mesh axis runs over, the one named last changes fastest.
Arguments:
- latent: float32 [1024, 512, 512], P(('chain', 'dist'), 'ang'), parts along dimension 0, may hold values from -6 to 6
- row_factor: bfloat16 [512, 512], replicated, may hold values from -0.25 to 0.25
- col_factor: bfloat16 [512, 512], replicated, may hold values from -0.25 to 0.25
- log_mean: float32 [1024], P(('chain', 'dist')), parts along dimension 0, may hold values from -6 to -4
- band_ratio: float32 [8], replicated, may hold values from 0.2 to 2
- star_counts: int32 [32, 16], P(('chain', 'ang', 'dist')), parts along dimension 0, may hold values from 16 to 128, as said below
- star_pixel: int32 [32, 16, 128], P(('chain', 'ang', 'dist')), parts along dimension 0, may hold values from 0 to 65535
- star_bin: int32 [32, 16, 128], P(('chain', 'ang', 'dist')), parts along dimension 0, may hold values from 0 to 127
- star_obs: float32 [32, 16, 8, 128], P(('chain', 'ang', 'dist')), parts along dimension 0, may hold values from 0 to 8
- star_isig: float32 [32, 16, 8, 128], P(('chain', 'ang', 'dist')), parts along dimension 0, may hold values from 0.5 to 5
Outputs:
- gradient: float32 [1024, 512, 512], P(('chain', 'dist'), 'ang'), parts along dimension 0
There are 2 independent parts, one for each index of `chain`. A program takes and returns all parts, laid end to end along the dimension named above; an argument that names none is the same for every part. Nothing has to cross between parts.
Inputs may be any that keep to these rules, and one draw needn't show every extreme that they name: The first star_counts[s, d] slots of a bucket hold stars, the rest are empty. In every draw one voxel owner has all 128 slots live from every star owner. `star_pixel`: Row-major index (column offset, row) within the 512 // 4 columns and 512 rows of the voxel owner. `star_bin`: offset within the voxel owner's 128 bins.
All inputs are finite; a program needn't handle non-finite values.
Results may differ from a plain program's by a relative error of at most 0.0062.
Values may be sent and summed in bfloat16 or wider, within the bound.
A program may use at most 320 MiB of HBM per device.

v0:
```python
import jax
import jax.numpy as jnp
from jax import lax
from jax.sharding import PartitionSpec as P


def nearer_sum(totals):
    every = lax.all_gather(totals[None], "dist", axis=0, tiled=True)
    position = jnp.arange(every.shape[0], dtype=jnp.int32)
    keep = position < lax.axis_index("dist")
    return jnp.sum(jnp.where(keep[:, None, None], every, 0.0), axis=0)


def farther_sum(totals):
    every = lax.all_gather(totals[None], "dist", axis=0, tiled=True)
    position = jnp.arange(every.shape[0], dtype=jnp.int32)
    keep = position > lax.axis_index("dist")
    return jnp.sum(jnp.where(keep[:, None, None], every, 0.0), axis=0)


def per_device(
    latent,
    row_factor,
    col_factor,
    log_mean,
    band_ratio,
    star_counts,
    star_pixel,
    star_bin,
    star_obs,
    star_isig,
):
    latent_bf = latent.astype(jnp.bfloat16)
    inner = jnp.einsum(
        "kab,cb->kca", latent_bf, col_factor, preferred_element_type=jnp.float32
    ).astype(jnp.bfloat16)
    field = jnp.einsum(
        "kca,ea->kce",
        lax.all_to_all(inner, "ang", split_axis=1, concat_axis=2, tiled=True),
        row_factor,
        preferred_element_type=jnp.float32,
    )
    density = jnp.exp(log_mean[:, None, None] + field)
    running = lax.cumsum(density, axis=0)
    extinction = running + nearer_sum(running[-1])[None]
    capacity = star_pixel.shape[-1]
    live = jnp.arange(capacity, dtype=jnp.int32)[None, None, :] < star_counts[:, :, None]
    weight = jnp.where(live[:, :, None, :], star_isig, 0.0)
    depth = star_obs.shape[2]
    pixel_in, bin_in = (
        lax.all_to_all(star_pixel, ("ang", "dist"), split_axis=1, concat_axis=0, tiled=True),
        lax.all_to_all(star_bin, ("ang", "dist"), split_axis=1, concat_axis=0, tiled=True),
    )
    first_in, second_in = (
        lax.all_to_all(star_obs, ("ang", "dist"), split_axis=1, concat_axis=0, tiled=True),
        lax.all_to_all(weight, ("ang", "dist"), split_axis=1, concat_axis=0, tiled=True),
    )
    pixel_in = pixel_in.reshape(-1, capacity)
    bin_in = bin_in.reshape(-1, capacity)
    first_in = first_in.reshape(-1, depth, capacity)
    second_in = second_in.reshape(-1, depth, capacity)
    block_pixels = extinction.shape[1] * extinction.shape[2]
    flat_index = bin_in * block_pixels + pixel_in
    predicted = extinction.reshape(-1)[flat_index]
    ratio = band_ratio[None, :, None]
    resid = (ratio * predicted[:, None, :] - first_in) * second_in
    coeff = jnp.sum(ratio * second_in * resid, axis=1)
    grad_ext = jnp.zeros((extinction.size,), jnp.float32)
    grad_ext = grad_ext.at[flat_index.reshape(-1)].add(coeff.reshape(-1)).reshape(extinction.shape)
    back_running = lax.cumsum(grad_ext, axis=0, reverse=True)
    grad_density = back_running + farther_sum(back_running[0])[None]
    grad_field = (grad_density * density).astype(jnp.bfloat16)
    back = jnp.einsum(
        "kce,ea->kca", grad_field, row_factor, preferred_element_type=jnp.float32
    ).astype(jnp.bfloat16)
    returned = lax.all_to_all(back, "ang", split_axis=2, concat_axis=1, tiled=True)
    adjoint = jnp.einsum("kca,cb->kab", returned, col_factor, preferred_element_type=jnp.float32)
    return latent + adjoint


def solution(mesh):
    in_specs = (
        P(("chain", "dist"), "ang", None),
        P(),
        P(),
        P(("chain", "dist")),
        P(),
        P(("chain", "ang", "dist"), None),
        P(("chain", "ang", "dist"), None, None),
        P(("chain", "ang", "dist"), None, None),
        P(("chain", "ang", "dist"), None, None, None),
        P(("chain", "ang", "dist"), None, None, None),
    )
    out_specs = P(("chain", "dist"), "ang", None)
    return jax.shard_map(
        per_device, mesh=mesh, in_specs=in_specs, out_specs=out_specs, check_vma=False
    )
```

profile of v0, /device:TPU:0, one launch (start us, length us, event | category | flops | bytes accessed | tf_op | source)
XLA Modules:
  0.0 1098.3 jit_solution(16854106347314775641)
XLA Ops:
  6.5 0.0 copy-start
  6.5 0.0 all-gather.3.cloned.1.call-start
  6.5 21.4 %convert_bitcast_fusion = bf16[128,512,128]{2,1,0:T(8,128)(2,1)} fusion(f32[128,128,512]{2,1,0:T(8,128)} %param.10, bf16[512,512]{1,0:T(8,128)(2,1)} %param.12), kind=kOutput, calls=%fused_computation.10 | convolution fusion | flops 8606711808 | bytes 50855936 | tf_op jit(solution)/shard_map/kab,cb->kca/dot_general | solution.py:34
  27.9 14.8 %copy.18 = bf16[128,512,128]{2,0,1:T(8,128)(2,1)S(1)} copy(bf16[128,512,128]{2,1,0:T(8,128)(2,1)} %convert_bitcast_fusion) | data formatting | bytes 33554432 | tf_op jit(solution)/shard_map/convert_element_type | solution.py:36
  42.7 187.0 %all_to_all.72 = bf16[128,512,128]{2,0,1:T(8,128)(2,1)S(1)} all-to-all(bf16[128,512,128]{2,0,1:T(8,128)(2,1)S(1)} %copy.18), channel_id=1, replica_groups=mesh['chain'=2,'ang'=4,'dist'=4] {'ang'}, dimensions={1} | all-to-all | bytes 33554432 | tf_op jit(solution)/shard_map/all_to_all | solution.py:39
  229.7 35.9 %copy.27 = bf16[128,4,128,128]{3,1,2,0:T(4,128)(2,1)} copy(bf16[128,4,128,128]{3,0,2,1:T(8,128)(2,1)S(1)} %bitcast.57) | data formatting | bytes 33554432 | tf_op jit(solution)/shard_map/all_to_all | solution.py:39
  265.7 24.9 %all_to_all.60 = bf16[128,128,512]{2,1,0:T(8,128)(2,1)} reshape(bf16[128,128,4,128]{3,2,1,0:T(4,128)(2,1)} %bitcast.58) | data formatting | bytes 33554432 | tf_op jit(solution)/shard_map/all_to_all | solution.py:39
  290.6 0.0 copy-done
  290.6 0.0 copy-start.3
  290.6 22.0 %fusion.13 = f32[128,128,512]{2,1,0:T(8,128)} fusion(bf16[128,128,512]{2,1,0:T(8,128)(2,1)} %all_to_all.60, bf16[512,512]{1,0:T(8,128)(2,1)S(1)} %copy-done), kind=kOutput, calls=%fused_computation.22 | convolution fusion | flops 8589934592 | bytes 50855936 | tf_op jit(solution)/shard_map/kca,ea->kce/dot_general | solution.py:37
  312.6 0.0 copy-done.3
  312.6 0.0 copy-start.5
  312.6 0.0 copy-start.2
  312.6 166.6 %fusion = f32[128,128,512]{2,1,0:T(8,128)} fusion(f32[128,128,512]{2,1,0:T(8,128)} %fusion.13, f32[128]{0:T(128)S(1)} %copy-done.3), kind=kOutput, calls=%fused_computation.4 | output fusion | flops 1073741824 | bytes 67109376 | tf_op jit(solution)/shard_map/per_device/reduce_window_sum | solution.py:44
  479.3 1.7 slice.10
  480.9 0.0 all-gather.3.cloned.1.call-update
  481.0 5.5 all-to-all-start
  486.5 0.0 copy-done.5
  486.5 0.1 iota_compare_fusion
  486.6 0.0 copy-done.2
  486.6 0.6 bitcast_select_fusion
  487.2 5.6 all-to-all-done
  492.8 3.5 all-to-all-start.1
  496.3 6.3 all-to-all-done.1
  502.6 3.5 all-to-all-start.2
  506.1 4.0 all-gather.3.cloned.1.call-done
  510.1 1.4 select_reduce_fusion.1
  511.5 1.2 all-to-all-done.2
  512.7 3.5 all-to-all-start.4
  516.2 0.0 all-gather.5.cloned.1.call-start
  516.2 24.6 %broadcast_add_fusion = f32[128,128,512]{2,1,0:T(8,128)} fusion(f32[128,128,512]{2,1,0:T(8,128)} %fusion, f32[128,512]{1,0:T(8,128)S(1)} %select_reduce_fusion.1), kind=kLoop, calls=%fused_computation.9 | loop fusion | flops 8388608 | bytes 67371008 | tf_op jit(solution)/shard_map/add | solution.py:45
  540.9 0.0 copy-start.4
  540.9 24.8 %copy.23 = f32[2048,4,8,128]{3,1,2,0:T(4,128)} copy(f32[2048,4,8,128]{3,2,1,0:T(8,128)} %bitcast.56) | data formatting | bytes 67108864
  565.7 24.5 %gather_fusion = f32[2048]{0:T(1024)S(1)} fusion(f32[8388608]{0:T(1024)} %bitcast.61, s32[2048]{0:T(1024)S(1)} %fusion.21), kind=kCustom, calls=%fused_computation | custom fusion | bytes 24576 | tf_op jit(solution)/shard_map/gather | solution.py:64
  590.2 0.0 all-to-all-done.4
  590.2 0.0 copy-done.4
  590.2 0.1 fusion.19
  590.3 24.4 %scatter_custom_fusion = f32[8388608]{0:T(1024)} fusion(s32[2048]{0:T(1024)S(1)} %bitcast.65, f32[2048]{0:T(1024)S(1)} %bitcast.64, f32[]{:T(128)} %constant.5.clone.1), kind=kCustom, calls=%fused_computation.15 | custom fusion | flops 2048 | bytes 33554436 | tf_op jit(solution)/shard_map/scatter-add | solution.py:69
  614.7 35.7 %reshape.146 = f32[128,128,512]{2,1,0:T(8,128)} reshape(f32[8388608]{0:T(1024)} %scatter_custom_fusion) | data formatting | bytes 67108864 | tf_op jit(solution)/shard_map/reshape | solution.py:69
  650.5 76.3 %fusion.22 = f32[128,128,512]{2,1,0:T(8,128)} fusion(f32[128,128,512]{2,1,0:T(8,128)} %reshape.146), kind=kOutput, calls=%fused_computation.40 | output fusion | flops 1065353216 | bytes 67108864 | tf_op jit(solution)/shard_map/per_device/reduce_window_sum | solution.py:70
  726.8 1.7 slice.11
  728.5 0.0 all-gather.5.cloned.1.call-update
  728.5 29.3 %all-gather.5.cloned.1.call-done = f32[4,128,512]{2,1,0:T(8,128)} async-done(((f32[1,128,512]{2,1,0:T(8,128)}), f32[4,128,512]{2,1,0:T(8,128)}) %all-gather.5.cloned.1.call-update) | async-done | bytes 1048592 | tf_op jit(solution)/shard_map/all_gather | solution.py:15
  757.8 1.4 select_reduce_fusion
  759.2 29.0 %fusion.11 = bf16[128,128,512]{2,1,0:T(8,128)(2,1)} fusion(f32[128,128,512]{2,1,0:T(8,128)} %fusion.22, f32[128,128,512]{2,1,0:T(8,128)} %fusion.13, f32[128,512]{1,0:T(8,128)S(1)} %select_reduce_fusion, f32[128]{0:T(128)S(1)} %copy-done.3, bf16[512,512]{1,0:T(8,128)(2,1)S(1)} %copy-done), kind=kOutput, calls=%fused_computation.17 | convolution fusion | flops 8631877632 | bytes 84673024 | tf_op jit(solution)/shard_map/kce,ea->kca/dot_general | solution.py:73
  788.3 23.5 %copy.21 = bf16[128,128,512]{1,0,2:T(8,128)(2,1)} copy(bf16[128,128,512]{2,1,0:T(8,128)(2,1)} %fusion.11) | data formatting | bytes 33554432 | tf_op jit(solution)/shard_map/convert_element_type | solution.py:75
  811.7 187.7 %all_to_all.73 = bf16[128,128,512]{1,0,2:T(8,128)(2,1)S(1)} all-to-all(bf16[128,128,512]{1,0,2:T(8,128)(2,1)} %copy.21), channel_id=1, replica_groups=mesh['chain'=2,'ang'=4,'dist'=4] {'ang'}, dimensions={2} | all-to-all | bytes 33554432 | tf_op jit(solution)/shard_map/all_to_all | solution.py:76
  999.4 0.0 copy-start.1
  999.4 35.9 %copy.26 = bf16[128,128,4,128]{1,2,3,0:T(4,128)(2,1)} copy(bf16[128,128,4,128]{1,0,3,2:T(8,128)(2,1)S(1)} %bitcast.59) | data formatting | bytes 33554432 | tf_op jit(solution)/shard_map/all_to_all | solution.py:76
  1035.4 24.9 %all_to_all.65 = bf16[128,512,128]{1,2,0:T(8,128)(2,1)} reshape(bf16[128,4,128,128]{2,1,3,0:T(4,128)(2,1)} %bitcast.60) | data formatting | bytes 33554432 | tf_op jit(solution)/shard_map/all_to_all | solution.py:76
  1060.3 0.0 copy-done.1
  1060.3 31.0 %convolution_add_fusion = f32[128,128,512]{2,1,0:T(8,128)} fusion(f32[128,128,512]{2,1,0:T(8,128)} %param.10, bf16[128,512,128]{1,2,0:T(8,128)(2,1)} %all_to_all.65, bf16[512,512]{1,0:T(8,128)(2,1)S(1)} %copy-done.1), kind=kOutput, calls=%fused_computation.18 | convolution fusion | flops 8598323200 | bytes 84410368 | tf_op jit(solution)/shard_map/kca,cb->kab/dot_general | solution.py:77
  (4 shorter events, 0.0 us)
Async XLA Ops:
  6.5 284.0 %copy-start = (bf16[512,512]{1,0:T(8,128)(2,1)S(1)}, bf16[512,512]{1,0:T(8,128)(2,1)}, u32[]{:S(2)}) copy-start(bf16[512,512]{1,0:T(8,128)(2,1)} %param.11) | copy-start | bytes 1572868
  6.5 503.6 %all-gather.3.cloned.1.call-start = ((), (), s32[]{:S(2)}) async-start(), calls=%async_computation.6 | async-start | bytes 1310720 | tf_op jit(solution)/shard_map/all_gather | solution.py:8
  290.6 22.0 %copy-start.3 = (f32[128]{0:T(128)S(1)}, f32[128]{0:T(128)}, u32[]{:S(2)}) copy-start(f32[128]{0:T(128)} %param.13) | copy-start | bytes 1540
  312.6 173.9 %copy-start.5 = (s32[1,16]{1,0:T(1,128)S(1)}, s32[1,16]{1,0:T(1,128)}, u32[]{:S(2)}) copy-start(s32[1,16]{1,0:T(1,128)} %param.15) | copy-start | bytes 196
  312.6 174.0 %copy-start.2 = (f32[1,16,8,128]{3,2,1,0:T(8,128)S(1)}, f32[1,16,8,128]{3,2,1,0:T(8,128)}, u32[]{:S(2)}) copy-start(f32[1,16,8,128]{3,2,1,0:T(8,128)} %param.19) | copy-start | bytes 196612
  481.0 11.8 %all-to-all-start = ((s32[1,16,128]{2,0,1:T(1,128)}), s32[1,16,128]{2,0,1:T(1,128)S(1)}, u32[]{:S(2)}, u32[]{:S(2)}) async-start(s32[1,16,128]{2,0,1:T(1,128)} %bitcast), calls=%async_computation | async-start | bytes 16384 | tf_op jit(solution)/shard_map/all_to_all | solution.py:52
  492.8 9.8 all-to-all-start.1
  502.6 10.1 all-to-all-start.2
  512.7 77.5 %all-to-all-start.4 = ((f32[1,16,8,128]{3,2,0,1:T(8,128)}), f32[1,16,8,128]{3,2,0,1:T(8,128)S(1)}, u32[]{:S(2)}, u32[]{:S(2)}) async-start(f32[1,16,8,128]{3,2,0,1:T(8,128)} %bitcast.15), calls=%async_computation.4 | async-start | bytes 131072 | tf_op jit(solution)/shard_map/all_to_all | solution.py:55
  516.2 241.6 %all-gather.5.cloned.1.call-start = ((), (), s32[]{:S(2)}) async-start(), calls=%async_computation.7 | async-start | bytes 1310720 | tf_op jit(solution)/shard_map/all_gather | solution.py:15
  540.9 49.3 %copy-start.4 = (f32[8]{0:T(128)S(1)}, f32[8]{0:T(128)}, u32[]{:S(2)}) copy-start(f32[8]{0:T(128)} %param.14) | copy-start | bytes 100
  999.4 60.8 %copy-start.1 = (bf16[512,512]{1,0:T(8,128)(2,1)S(1)}, bf16[512,512]{1,0:T(8,128)(2,1)}, u32[]{:S(2)}) copy-start(bf16[512,512]{1,0:T(8,128)(2,1)} %param.12) | copy-start | bytes 1572868
Sparse Core Ops, SparseCore 0:
  481.1 28.9 all-gather.2
  728.6 29.1 all-gather.4
where the time goes:
time: 1120 us; the launch traced here: 1100 us
  blocking collectives  375 us (33%)
  other arithmetic  296 us (26%)
  local copies, waits for them, and re-layouts  248 us (22%)
  matrix products  103 us (9%)
  waiting for transfers between devices  46.3 us (4%)
  starting transfers between devices  16 us (1%)
  between operations  13.7 us (1%)
    all_to_all x1, blocking collectives, per_device(): lax.all_to_all(back, 'ang', split_axis=2, concat_axis=1, tiled=True)  188 us
    all_to_all x1, blocking collectives, per_device(): lax.all_to_all(inner, 'ang', split_axis=1, concat_axis=2, tiled=True)  187 us
    another operation x1, other arithmetic, per_device(): running = lax.cumsum(density, axis=0)  167 us
    another operation x1, other arithmetic, per_device(): back_running = lax.cumsum(grad_ext, axis=0, reverse=True)  76.3 us
    all_to_all x2, local copies, waits for them, and re-layouts, per_device(): lax.all_to_all(inner, 'ang', split_axis=1, concat_axis=2, tiled=True)  60.8 us
    all_to_all x2, local copies, waits for them, and re-layouts, per_device(): lax.all_to_all(back, 'ang', split_axis=2, concat_axis=1, tiled=True)  60.8 us
    reshape x1, local copies, waits for them, and re-layouts, per_device(): grad_ext.at[flat_index.reshape(-1)].add(coeff.reshape(-1))  35.7 us
    dot_general x1, matrix products, per_device(): jnp.einsum('kca,cb->kab', returned, col_factor, preferred_element_type=jn...  31 us
  transfers between devices with their start and end apart: 6, of which 5 were waited for; matrix products, arithmetic and copies ran while one was open for 7% of the time, Pallas kernels for 0%

commit v1 on v0

--- a/solution.py
+++ b/solution.py
@@ -1,7 +1,16 @@
+import functools
+
 import jax
 import jax.numpy as jnp
 from jax import lax
+from jax.experimental import pallas as pl
+from jax.experimental.pallas import tpu as pltpu
 from jax.sharding import PartitionSpec as P
+
+LANES = 128
+CHUNKS = 4
+STEP = 8
+VMEM = 48 << 20
 
 
 def nearer_sum(totals):
@@ -18,7 +27,7 @@
     return jnp.sum(jnp.where(keep[:, None, None], every, 0.0), axis=0)
 
 
-def per_device(
+def general(
     latent,
     row_factor,
     col_factor,
@@ -78,6 +87,253 @@
     return latent + adjoint
 
 
+def dot_nt(x, y):
+    return lax.dot_general(x, y, (((1,), (1,)), ((), ())), preferred_element_type=jnp.float32)
+
+
+def split_store(product, out_refs):
+    for block, out_ref in enumerate(out_refs):
+        for k in range(out_ref.shape[0]):
+            out_ref[k] = product[
+                block * LANES : (block + 1) * LANES, k * LANES : (k + 1) * LANES
+            ].astype(out_ref.dtype)
+
+
+def joined(refs):
+    return jnp.concatenate([ref[...].reshape(-1, LANES) for ref in refs], axis=1)
+
+
+def column_kernel(latent_ref, col_ref, *out_refs):
+    block = latent_ref[...].astype(jnp.bfloat16).reshape(-1, latent_ref.shape[2])
+    split_store(dot_nt(col_ref[...], block), out_refs)
+
+
+def density_kernel(parts, chained, mean_ref, row_ref, start_ref, *refs):
+    in_refs = refs[:parts]
+    running_ref, density_ref, total_ref = refs[parts + (2 if chained else 0) :]
+    step = pl.program_id(0)
+
+    @pl.when(step == 0)
+    def _():
+        total_ref[...] = start_ref[...]
+
+    field = dot_nt(joined(in_refs), row_ref[...])
+    for slab in range(field.shape[1] // LANES):
+        rows = slice(slab * LANES, (slab + 1) * LANES)
+        total = total_ref[rows]
+        for k in range(STEP):
+            density = jnp.exp(mean_ref[step * STEP + k] + field[k * LANES : (k + 1) * LANES, rows])
+            total = total + density
+            running_ref[k, rows] = total
+            density_ref[k, rows] = density.astype(density_ref.dtype)
+        total_ref[rows] = total
+
+
+def adjoint_kernel(row_ref, start_ref, grad_ref, density_ref, *refs):
+    *out_refs, total_ref, field_ref = refs
+
+    @pl.when(pl.program_id(0) == 0)
+    def _():
+        total_ref[...] = start_ref[...]
+
+    for slab in range(total_ref.shape[0] // LANES):
+        rows = slice(slab * LANES, (slab + 1) * LANES)
+        total = total_ref[rows]
+        for k in reversed(range(STEP)):
+            total = total + grad_ref[k, rows]
+            field_ref[k * LANES : (k + 1) * LANES, rows] = (
+                total * density_ref[k, rows].astype(jnp.float32)
+            ).astype(jnp.bfloat16)
+        total_ref[rows] = total
+    split_store(dot_nt(row_ref[...], field_ref[...]), out_refs)
+
+
+def output_kernel(parts, latent_ref, col_ref, *refs):
+    in_refs, out_ref = refs[:parts], refs[-1]
+    adjoint = jnp.dot(joined(in_refs), col_ref[...], preferred_element_type=jnp.float32)
+    out_ref[...] = latent_ref[...] + adjoint.reshape(out_ref.shape)
+
+
+def call(kernel, cost, **kwargs):
+    return pl.pallas_call(
+        kernel,
+        compiler_params=pltpu.CompilerParams(vmem_limit_bytes=VMEM),
+        cost_estimate=pl.CostEstimate(flops=cost[0], bytes_accessed=cost[1], transcendentals=0),
+        **kwargs,
+    )
+
+
+def exchange(parts):
+    count = len(parts)
+    return [parts[0]] + [
+        lax.ppermute(parts[b], "ang", [(i, i ^ b) for i in range(count)]) for b in range(1, count)
+    ]
+
+
+def masked_sum(totals, nearer):
+    every = lax.all_gather(totals[None], "dist", axis=0, tiled=True)
+    position = jnp.arange(every.shape[0], dtype=jnp.int32)
+    me = lax.axis_index("dist")
+    keep = position < me if nearer else position > me
+    return jnp.sum(jnp.where(keep[:, None, None], every, 0.0), axis=0)
+
+
+def fused(
+    parts,
+    latent,
+    row_factor,
+    col_factor,
+    log_mean,
+    band_ratio,
+    star_counts,
+    star_pixel,
+    star_bin,
+    star_obs,
+    star_isig,
+):
+    bins, rows, cols = latent.shape
+    all_rows = rows * parts
+    slabs = all_rows // LANES
+    pixel_rows = slabs * LANES
+    me = lax.axis_index("ang")
+    order = me ^ jnp.arange(parts, dtype=jnp.int32)
+    col_order = col_factor.reshape(parts, LANES, cols)[order].reshape(cols, cols)
+    row_order = (
+        row_factor.reshape(all_rows, parts, LANES)[:, order].reshape(all_rows, all_rows)
+    )
+    row_turned = row_order.T
+
+    capacity = star_pixel.shape[-1]
+    live = jnp.arange(capacity, dtype=jnp.int32)[None, None, :] < star_counts[:, :, None]
+    ratio = band_ratio[None, None, :, None]
+    pull = ratio * jnp.where(live[:, :, None, :], star_isig, 0.0) ** 2
+    slope = jnp.sum(pull * ratio, axis=2)
+    offset = jnp.sum(pull * star_obs, axis=2)
+    star_row = star_pixel % all_rows
+    pixel = ((star_row // LANES) * LANES + star_pixel // all_rows) * LANES + star_row % LANES
+    block_pixels = pixel_rows * LANES
+    voxel = star_bin * block_pixels + pixel
+    packed = jnp.stack([voxel.astype(jnp.float32), slope, offset], axis=2)
+    packed = lax.all_to_all(packed, ("ang", "dist"), split_axis=1, concat_axis=0, tiled=True)
+    packed = packed.reshape(-1, 3, capacity)
+    voxel = packed[:, 0].astype(jnp.int32).reshape(-1)
+    slope, offset = packed[:, 1].reshape(-1), packed[:, 2].reshape(-1)
+    pixel = voxel % block_pixels
+    at_row = (pixel[:, None] // LANES == jnp.arange(pixel_rows)[None]).astype(jnp.float32)
+    at_lane = (pixel[:, None] % LANES == jnp.arange(LANES)[None]).astype(jnp.float32)
+
+    chunk = bins // CHUNKS
+    steps = chunk // STEP
+    flops = 2 * chunk * rows * cols * all_rows
+    whole = lambda shape: pl.BlockSpec(shape, lambda i: (0,) * len(shape))
+    piece = pl.BlockSpec((STEP, LANES, LANES), lambda i: (i, 0, 0))
+    pieces = [jax.ShapeDtypeStruct((chunk, LANES, LANES), jnp.bfloat16)] * parts
+    anywhere = pl.BlockSpec(memory_space=pl.ANY)
+
+    def placed(shape, c, back=False):
+        if back:
+            return pl.BlockSpec(shape, lambda i: (c * steps + steps - 1 - i, 0, 0))
+        return pl.BlockSpec(shape, lambda i: (c * steps + i, 0, 0))
+
+    latent_block = (STEP, rows, cols)
+    pixel_block = (STEP, pixel_rows, LANES)
+
+    arrived = []
+    for c in range(CHUNKS):
+        sent = call(
+            column_kernel,
+            (flops, chunk * rows * cols * 6),
+            grid=(steps,),
+            in_specs=[placed(latent_block, c), whole((cols, cols))],
+            out_specs=[piece] * parts,
+            out_shape=pieces,
+        )(latent, col_order)
+        arrived.append(exchange(sent))
+
+    kept = []
+    total = jnp.zeros((pixel_rows, LANES), jnp.float32)
+    for c in range(CHUNKS):
+        *kept, total = call(
+            functools.partial(density_kernel, parts, c > 0),
+            (flops, chunk * rows * cols * 8),
+            grid=(steps,),
+            in_specs=[
+                pl.BlockSpec(memory_space=pltpu.SMEM),
+                whole((all_rows, all_rows)),
+                whole((pixel_rows, LANES)),
+            ]
+            + [piece] * parts
+            + [anywhere] * len(kept),
+            out_specs=[
+                placed(pixel_block, c),
+                placed(pixel_block, c),
+                whole((pixel_rows, LANES)),
+            ],
+            out_shape=[
+                jax.ShapeDtypeStruct((bins, pixel_rows, LANES), jnp.float32),
+                jax.ShapeDtypeStruct((bins, pixel_rows, LANES), jnp.bfloat16),
+                jax.ShapeDtypeStruct((pixel_rows, LANES), jnp.float32),
+            ],
+            input_output_aliases={3 + parts + n: n for n in range(len(kept))},
+        )(log_mean[c * chunk : (c + 1) * chunk], row_order, total, *arrived[c], *kept)
+    running, density = kept
+
+    exact = lax.Precision.HIGHEST
+    nearer = masked_sum(total, True)
+    before = jnp.sum(jnp.dot(at_row, nearer, precision=exact) * at_lane, axis=1)
+    predicted = running.reshape(-1)[voxel] + before
+    coeff = slope * predicted - offset
+    grad_ext = jnp.zeros((bins * block_pixels,), jnp.float32).at[voxel].add(coeff)
+    grad_ext = grad_ext.reshape(bins, pixel_rows, LANES)
+    own = lax.dot_general(
+        at_row, at_lane * coeff[:, None], (((0,), (0,)), ((), ())), precision=exact
+    )
+    total = masked_sum(own, False)
+
+    arrived = [None] * CHUNKS
+    for c in reversed(range(CHUNKS)):
+        *sent, total = call(
+            adjoint_kernel,
+            (flops, chunk * rows * cols * 8),
+            grid=(steps,),
+            in_specs=[
+                whole((all_rows, all_rows)),
+                whole((pixel_rows, LANES)),
+                placed(pixel_block, c, True),
+                placed(pixel_block, c, True),
+            ],
+            out_specs=[pl.BlockSpec((STEP, LANES, LANES), lambda i: (steps - 1 - i, 0, 0))]
+            * parts
+            + [whole((pixel_rows, LANES))],
+            out_shape=pieces + [jax.ShapeDtypeStruct((pixel_rows, LANES), jnp.float32)],
+            scratch_shapes=[pltpu.VMEM((STEP * LANES, all_rows), jnp.bfloat16)],
+        )(row_turned, total, grad_ext, density)
+        arrived[c] = exchange(sent)
+
+    out = []
+    for c in reversed(range(CHUNKS)):
+        out = call(
+            functools.partial(output_kernel, parts),
+            (flops, chunk * rows * cols * 10),
+            grid=(steps,),
+            in_specs=[placed(latent_block, c), whole((cols, cols))]
+            + [piece] * parts
+            + [anywhere] * len(out),
+            out_specs=[placed(latent_block, c)],
+            out_shape=[jax.ShapeDtypeStruct((bins, rows, cols), jnp.float32)],
+            input_output_aliases={2 + parts + n: n for n in range(len(out))},
+        )(latent, col_order, *arrived[c], *out)
+    return out[0]
+
+
+def per_device(parts, latent, *others):
+    bins, rows, cols = latent.shape
+    tiles = rows == LANES and cols == parts * LANES and bins % (CHUNKS * STEP) == 0
+    if tiles and parts & (parts - 1) == 0 and bins * rows * cols <= 1 << 24:
+        return fused(parts, latent, *others)
+    return general(latent, *others)
+
+
 def solution(mesh):
     in_specs = (
         P(("chain", "dist"), "ang", None),
@@ -93,5 +349,5 @@
     )
     out_specs = P(("chain", "dist"), "ang", None)
     return jax.shard_map(
-        per_device, mesh=mesh, in_specs=in_specs, out_specs=out_specs, check_vma=False
-    )
+        functools.partial(per_device, mesh.shape["ang"]), mesh=mesh, in_specs=in_specs, out_specs=out_specs, check_vma=False
+    )

time: 1120 us -> 503 us (0.45); the launches traced: 1100 us -> 501 us
  blocking collectives: 375 us -> 0 us
  other arithmetic: 296 us -> 28.7 us
  waiting for transfers between devices: 46.3 us -> 268 us
  local copies, waits for them, and re-layouts: 248 us -> 40 us
  Pallas kernels: 0 us -> 118 us
  matrix products: 103 us -> 6.14 us
    all_to_all x2 -> x0, blocking collectives: 375 us -> none  [the longest x1 188 us: per_device(): lax.all_to_all(back, 'ang', split_axis=2, concat_axis=1, tiled=True)]
    ppermute x0 -> x24, waiting for transfers between devices: none -> 261 us  [exchange(): lax.ppermute(parts[b], 'ang', [(i, i ^ b) for i in range(count)])]
    another operation x2 -> x1, other arithmetic: 243 us -> 0.62 us  [fused(): packed = jnp.stack([voxel.astype(jnp.float32), slope, offset], axis=2)]
    all_to_all x4 -> x1, local copies, waits for them, and re-layouts: 122 us -> 0.01 us  [fused(): lax.all_to_all(packed, ('ang', 'dist'), split_axis=1, concat_axis=0, tile...]
    pallas_call x0 -> x16, Pallas kernels: none -> 118 us  [the longest x4 33.2 us: fused(): call(functools.partial(output_kernel, parts), (flops, chunk * rows * cols...]
    dot_general x4 -> x2, matrix products: 103 us -> 6.14 us  [the longest x1 3.43 us: fused(): lax.dot_general(at_row, at_lane * coeff[:, None], (((0,), (0,)), ((), ())...]
    convert_element_type x2 -> x0, local copies, waits for them, and re-layouts: 38.2 us -> none  [the longest x1 23.5 us: per_device(): back = jnp.einsum('kce,ea->kca', grad_field, row_factor, preferred_elemen...]
    reshape x1 -> x2, local copies, waits for them, and re-layouts: 35.7 us -> 0.48 us  [fused(): row_factor.reshape(all_rows, parts, LANES)[:, order]]
  transfers between devices with their start and end apart: 6 -> 27, of which waited for: 5 -> 18; matrix products, arithmetic and copies ran while one was open for 7% -> 11% of each run, Pallas kernels for 0% -> 15%
where the time goes in v1:
time: 503 us; the launch traced here: 501 us
  waiting for transfers between devices  268 us (53%)
  Pallas kernels  118 us (23%)
  local copies, waits for them, and re-layouts  40 us (8%)
  other arithmetic  28.7 us (6%)
  starting transfers between devices  26.9 us (5%)
  between operations  13.7 us (3%)
  matrix products  6.14 us (1%)
    ppermute x24, waiting for transfers between devices, exchange(): lax.ppermute(parts[b], 'ang', [(i, i ^ b) for i in range(count)])  261 us
    pallas_call x4, Pallas kernels, fused(): call(functools.partial(output_kernel, parts), (flops, chunk * rows * cols...  33.2 us
    pallas_call x4, Pallas kernels, fused(): call(adjoint_kernel, (flops, chunk * rows * cols * 8), grid=(steps,), in_...  29.9 us
    pallas_call x4, Pallas kernels, fused(): call(functools.partial(density_kernel, parts, c > 0), (flops, chunk * row...  28.6 us
    gather x1, local copies, waits for them, and re-layouts, fused(): predicted = running.reshape(-1)[voxel] + before  26.4 us
    pallas_call x4, Pallas kernels, fused(): call(column_kernel, (flops, chunk * rows * cols * 6), grid=(steps,), in_s...  26 us
    scatter-add x1, other arithmetic, fused(): jnp.zeros((bins * block_pixels,), jnp.float32).at[voxel].add(coeff)  25 us
    ppermute x24, starting transfers between devices, exchange(): lax.ppermute(parts[b], 'ang', [(i, i ^ b) for i in range(count)])  20.7 us
  transfers between devices with their start and end apart: 27, of which 18 were waited for; matrix products, arithmetic and copies ran while one was open for 11% of the time, Pallas kernels for 15%

profile of v1, /device:TPU:0, one launch (start us, length us, event | category | flops | bytes accessed | tf_op | source)
XLA Modules:
  0.0 501.0 jit_solution(16075322247778563865)
XLA Ops:
  6.6 1.0 copy-done
  8.2 6.4 %shard_map.100 = (bf16[32,128,128]{2,1,0:T(8,128)(2,1)S(1)}, bf16[32,128,128]{2,1,0:T(8,128)(2,1)S(1)}, bf16[32,128,128]{2,1,0:T(8,128)(2,1)S(1)}, bf16[32,128,128]{2,1,0:T(8,128)(2,1)}) custom-call(f32[128,128,512]{2,1,0:T(8,128)} %latent_ref.15, bf16[512,512]{1,0:T(8,128)(2,1)S(1)} %bitcast.42), custom_call_target="tpu_custom_call" | custom-call | flops 2147483648 | bytes 12582912 | tf_op jit(solution)/shard_map/pallas_call | solution.py:243
  14.6 1.0 copy-done.6
  16.0 2.5 collective-permute-start.1
  18.7 6.8 %shard_map.102 = (bf16[32,128,128]{2,1,0:T(8,128)(2,1)S(1)}, bf16[32,128,128]{2,1,0:T(8,128)(2,1)}, bf16[32,128,128]{2,1,0:T(8,128)(2,1)}, bf16[32,128,128]{2,1,0:T(8,128)(2,1)}) custom-call(f32[128,128,512]{2,1,0:T(8,128)} %latent_ref.15, bf16[512,512]{1,0:T(8,128)(2,1)S(1)} %bitcast.43), custom_call_target="tpu_custom_call" | custom-call | flops 2147483648 | bytes 12582912 | tf_op jit(solution)/shard_map/pallas_call | solution.py:243
  25.5 1.0 copy-done.4
  26.6 1.8 collective-permute-start.4
  28.4 6.3 %shard_map.104 = (bf16[32,128,128]{2,1,0:T(8,128)(2,1)S(1)}, bf16[32,128,128]{2,1,0:T(8,128)(2,1)}, bf16[32,128,128]{2,1,0:T(8,128)(2,1)S(1)}, bf16[32,128,128]{2,1,0:T(8,128)(2,1)S(1)}) custom-call(f32[128,128,512]{2,1,0:T(8,128)} %latent_ref.15, bf16[512,512]{1,0:T(8,128)(2,1)S(1)} %bitcast.44), custom_call_target="tpu_custom_call" | custom-call | flops 2147483648 | bytes 12582912 | tf_op jit(solution)/shard_map/pallas_call | solution.py:243
  34.7 1.0 copy-done.10
  35.7 1.0 copy-done.13
  36.7 1.0 copy-done.8
  37.7 4.9 collective-permute-done.1.refs_2_
  42.6 1.0 copy-done.11
  44.0 0.7 gather_fusion.1
  45.2 19.6 %collective-permute-done.2.refs_3_ = bf16[32,128,128]{2,1,0:T(8,128)(2,1)} collective-permute-done((bf16[32,128,128]{2,1,0:T(8,128)(2,1)}, bf16[32,128,128]{2,1,0:T(8,128)(2,1)}, u32[]{:S(2)}, u32[]{:S(2)}) %collective-permute-start.2) | collective-permute-done | bytes 1048608 | tf_op jit(solution)/shard_map/ppermute | solution.py:169
  64.8 1.6 collective-permute-start.7
  66.5 6.5 %shard_map.106 = (bf16[32,128,128]{2,1,0:T(8,128)(2,1)S(1)}, bf16[32,128,128]{2,1,0:T(8,128)(2,1)}, bf16[32,128,128]{2,1,0:T(8,128)(2,1)}, bf16[32,128,128]{2,1,0:T(8,128)(2,1)S(1)}) custom-call(f32[128,128,512]{2,1,0:T(8,128)} %latent_ref.15, bf16[512,512]{1,0:T(8,128)(2,1)S(1)} %bitcast.45), custom_call_target="tpu_custom_call" | custom-call | flops 2147483648 | bytes 12582912 | tf_op jit(solution)/shard_map/pallas_call | solution.py:243
  73.1 14.6 %collective-permute-done.4.refs_2_ = bf16[32,128,128]{2,1,0:T(8,128)(2,1)} collective-permute-done((bf16[32,128,128]{2,1,0:T(8,128)(2,1)}, bf16[32,128,128]{2,1,0:T(8,128)(2,1)}, u32[]{:S(2)}, u32[]{:S(2)}) %collective-permute-start.4) | collective-permute-done | bytes 1048608 | tf_op jit(solution)/shard_map/ppermute | solution.py:169
  87.6 22.1 %collective-permute-done.5.refs_3_ = bf16[32,128,128]{2,1,0:T(8,128)(2,1)} collective-permute-done((bf16[32,128,128]{2,1,0:T(8,128)(2,1)}, bf16[32,128,128]{2,1,0:T(8,128)(2,1)}, u32[]{:S(2)}, u32[]{:S(2)}) %collective-permute-start.5) | collective-permute-done | bytes 1048608 | tf_op jit(solution)/shard_map/ppermute | solution.py:169
  109.7 1.6 collective-permute-start.10
  111.7 1.2 copy-done.9
  112.9 7.1 %shard_map.101 = (f32[128,512,128]{2,1,0:T(8,128)}, bf16[128,512,128]{2,1,0:T(8,128)(2,1)}, f32[512,128]{1,0:T(8,128)S(1)}) custom-call(f32[32]{0:T(128)S(1)} %get-tuple-element.103.mean_ref, bf16[512,512]{1,0:T(8,128)(2,1)S(1)} %copy.57.row_ref, f32[512,128]{1,0:T(8,128)S(1)} %broadcast_in_dim.60.start_ref, bf16[32,128,128]{2,1,0:T(8,128)(2,1)S(1)} %copy-done.7, ...), custom_call_target="tpu_custom_call" | custom-call | flops 2147483648 | bytes 16777216 | tf_op jit(solution)/shard_map/pallas_call | solution.py:256
  120.0 7.9 %shard_map.103 = (f32[128,512,128]{2,1,0:T(8,128)}, bf16[128,512,128]{2,1,0:T(8,128)(2,1)}, f32[512,128]{1,0:T(8,128)S(1)}) custom-call(f32[32]{0:T(128)S(1)} %get-tuple-element.106.mean_ref, bf16[512,512]{1,0:T(8,128)(2,1)S(1)} %copy.57.row_ref, f32[512,128]{1,0:T(8,128)S(1)} %get-tuple-element.56.start_ref, ...), custom_call_target="tpu_custom_call", output_to_operand_aliasing={{0}: (7, {}), {1}: (8, {})} | custom-call | flops 2147483648 | bytes 16777216 | tf_op jit(solution)/shard_map/pallas_call | solution.py:256
  127.9 4.6 collective-permute-done.7.refs_2_
  132.4 22.1 %collective-permute-done.8.refs_3_ = bf16[32,128,128]{2,1,0:T(8,128)(2,1)S(1)} collective-permute-done((bf16[32,128,128]{2,1,0:T(8,128)(2,1)}, bf16[32,128,128]{2,1,0:T(8,128)(2,1)S(1)}, u32[]{:S(2)}, u32[]{:S(2)}) %collective-permute-start.8) | collective-permute-done | bytes 1048608 | tf_op jit(solution)/shard_map/ppermute | solution.py:169
  154.6 7.1 %shard_map.105 = (f32[128,512,128]{2,1,0:T(8,128)}, bf16[128,512,128]{2,1,0:T(8,128)(2,1)}, f32[512,128]{1,0:T(8,128)S(1)}) custom-call(f32[32]{0:T(128)S(1)} %get-tuple-element.104.mean_ref, bf16[512,512]{1,0:T(8,128)(2,1)S(1)} %copy.57.row_ref, f32[512,128]{1,0:T(8,128)S(1)} %get-tuple-element.63.start_ref, ...), custom_call_target="tpu_custom_call", output_to_operand_aliasing={{0}: (7, {}), {1}: (8, {})} | custom-call | flops 2147483648 | bytes 16777216 | tf_op jit(solution)/shard_map/pallas_call | solution.py:256
  161.7 15.7 %collective-permute-done.10.refs_2_ = bf16[32,128,128]{2,1,0:T(8,128)(2,1)S(1)} collective-permute-done((bf16[32,128,128]{2,1,0:T(8,128)(2,1)}, bf16[32,128,128]{2,1,0:T(8,128)(2,1)S(1)}, u32[]{:S(2)}, u32[]{:S(2)}) %collective-permute-start.10) | collective-permute-done | bytes 1048608 | tf_op jit(solution)/shard_map/ppermute | solution.py:169
  177.4 22.1 %collective-permute-done.11.refs_3_ = bf16[32,128,128]{2,1,0:T(8,128)(2,1)S(1)} collective-permute-done((bf16[32,128,128]{2,1,0:T(8,128)(2,1)S(1)}, bf16[32,128,128]{2,1,0:T(8,128)(2,1)S(1)}, u32[]{:S(2)}, u32[]{:S(2)}) %collective-permute-start.11) | collective-permute-done | bytes 1048608 | tf_op jit(solution)/shard_map/ppermute | solution.py:169
  199.5 6.6 %shard_map.107 = (f32[128,512,128]{2,1,0:T(8,128)}, bf16[128,512,128]{2,1,0:T(8,128)(2,1)}, f32[512,128]{1,0:T(8,128)}) custom-call(f32[32]{0:T(128)S(1)} %get-tuple-element.105.mean_ref, bf16[512,512]{1,0:T(8,128)(2,1)S(1)} %copy.57.row_ref, f32[512,128]{1,0:T(8,128)S(1)} %get-tuple-element.70.start_ref, ...), custom_call_target="tpu_custom_call", output_to_operand_aliasing={{0}: (7, {}), {1}: (8, {})} | custom-call | flops 2147483648 | bytes 16777216 | tf_op jit(solution)/shard_map/pallas_call | solution.py:256
  206.9 6.0 %all-to-all-start = ((f32[1,16,3,128]{3,0,2,1:T(1,128)}), f32[1,16,3,128]{3,0,2,1:T(1,128)S(1)}, u32[]{:S(2)}, u32[]{:S(2)}) async-start(f32[1,16,3,128]{3,0,2,1:T(1,128)} %pad_maximum_fusion), calls=%async_computation | async-start | bytes 49152 | tf_op jit(solution)/shard_map/all_to_all | solution.py:217
  213.1 6.2 %all-to-all-done = f32[1,16,3,128]{3,0,2,1:T(1,128)S(1)} async-done(((f32[1,16,3,128]{3,0,2,1:T(1,128)}), f32[1,16,3,128]{3,0,2,1:T(1,128)S(1)}, u32[]{:S(2)}, u32[]{:S(2)}) %all-to-all-start) | async-done | bytes 24608 | tf_op jit(solution)/shard_map/all_to_all | solution.py:217
  219.4 26.4 %gather_fusion.2 = f32[2048]{0:T(1024)S(1)} fusion(f32[8388608]{0:T(1024)} %bitcast.59, s32[2048]{0:T(1024)S(1)} %broadcast_clamp_fusion), kind=kCustom, calls=%fused_computation.2 | custom fusion | bytes 24576 | tf_op jit(solution)/shard_map/gather | solution.py:284
  245.8 1.4 select_reduce_fusion.1
  247.2 2.7 fusion.9
  249.9 3.4 fusion.5
  253.4 25.0 %scatter_custom_fusion = f32[8388608]{0:T(1024)} fusion(s32[2048]{0:T(1024)S(1)} %bitcast.68, f32[2048]{0:T(1024)S(1)} %fusion.21, f32[]{:T(128)} %constant.97.clone.1), kind=kCustom, calls=%fused_computation.4 | custom fusion | flops 2048 | bytes 33554436 | tf_op jit(solution)/shard_map/scatter-add | solution.py:286
  278.9 1.4 select_reduce_fusion.start_ref
  280.3 8.0 %shard_map.108 = (bf16[32,128,128]{2,1,0:T(8,128)(2,1)S(1)}, bf16[32,128,128]{2,1,0:T(8,128)(2,1)}, bf16[32,128,128]{2,1,0:T(8,128)(2,1)}, bf16[32,128,128]{2,1,0:T(8,128)(2,1)}, f32[512,128]{1,0:T(8,128)S(1)}) custom-call(bf16[512,512]{1,0:T(8,128)(2,1)S(1)} %bitcast.51, f32[512,128]{1,0:T(8,128)S(1)} %select_reduce_fusion.start_ref, ...), custom_call_target="tpu_custom_call" | custom-call | flops 2147483648 | bytes 16777216 | tf_op jit(solution)/shard_map/pallas_call | solution.py:295
  288.3 6.7 %shard_map.109 = (bf16[32,128,128]{2,1,0:T(8,128)(2,1)S(1)}, bf16[32,128,128]{2,1,0:T(8,128)(2,1)S(1)}, bf16[32,128,128]{2,1,0:T(8,128)(2,1)S(1)}, bf16[32,128,128]{2,1,0:T(8,128)(2,1)S(1)}, f32[512,128]{1,0:T(8,128)S(1)}) custom-call(bf16[512,512]{1,0:T(8,128)(2,1)S(1)} %bitcast.52, f32[512,128]{1,0:T(8,128)S(1)} %get-tuple-element.80.start_ref, ...), custom_call_target="tpu_custom_call" | custom-call | flops 2147483648 | bytes 16777216 | tf_op jit(solution)/shard_map/pallas_call | solution.py:295
  294.9 7.5 %shard_map.110 = (bf16[32,128,128]{2,1,0:T(8,128)(2,1)S(1)}, bf16[32,128,128]{2,1,0:T(8,128)(2,1)S(1)}, bf16[32,128,128]{2,1,0:T(8,128)(2,1)}, bf16[32,128,128]{2,1,0:T(8,128)(2,1)S(1)}, f32[512,128]{1,0:T(8,128)S(1)}) custom-call(bf16[512,512]{1,0:T(8,128)(2,1)S(1)} %bitcast.53, f32[512,128]{1,0:T(8,128)S(1)} %get-tuple-element.81.start_ref, ...), custom_call_target="tpu_custom_call" | custom-call | flops 2147483648 | bytes 16777216 | tf_op jit(solution)/shard_map/pallas_call | solution.py:295
  302.9 1.5 collective-permute-start.19
  304.4 0.7 collective-permute-start.21
  305.1 1.5 collective-permute-start.22
  306.6 1.2 collective-permute-start.23
  307.8 21.2 %collective-permute-done.19.refs_2_ = bf16[32,128,128]{2,1,0:T(8,128)(2,1)S(1)} collective-permute-done((bf16[32,128,128]{2,1,0:T(8,128)(2,1)S(1)}, bf16[32,128,128]{2,1,0:T(8,128)(2,1)S(1)}, u32[]{:S(2)}, u32[]{:S(2)}) %collective-permute-start.19) | collective-permute-done | bytes 1048608 | tf_op jit(solution)/shard_map/ppermute | solution.py:169
  329.0 1.5 collective-permute-start.16
  330.4 20.0 %collective-permute-done.20.refs_3_ = bf16[32,128,128]{2,1,0:T(8,128)(2,1)S(1)} collective-permute-done((bf16[32,128,128]{2,1,0:T(8,128)(2,1)S(1)}, bf16[32,128,128]{2,1,0:T(8,128)(2,1)S(1)}, u32[]{:S(2)}, u32[]{:S(2)}) %collective-permute-start.20) | collective-permute-done | bytes 1048608 | tf_op jit(solution)/shard_map/ppermute | solution.py:169
  350.4 1.9 collective-permute-start.17
  352.3 7.8 %shard_map.111 = (bf16[32,128,128]{2,1,0:T(8,128)(2,1)S(1)}, bf16[32,128,128]{2,1,0:T(8,128)(2,1)S(1)}, bf16[32,128,128]{2,1,0:T(8,128)(2,1)}, bf16[32,128,128]{2,1,0:T(8,128)(2,1)}, f32[512,128]{1,0:T(8,128)}) custom-call(bf16[512,512]{1,0:T(8,128)(2,1)S(1)} %bitcast.54, f32[512,128]{1,0:T(8,128)S(1)} %get-tuple-element.82.start_ref, ...), custom_call_target="tpu_custom_call" | custom-call | flops 2147483648 | bytes 16777216 | tf_op jit(solution)/shard_map/pallas_call | solution.py:295
  360.1 1.0 copy-done.14
  361.1 12.9 %collective-permute-done.22.refs_2_ = bf16[32,128,128]{2,1,0:T(8,128)(2,1)} collective-permute-done((bf16[32,128,128]{2,1,0:T(8,128)(2,1)}, bf16[32,128,128]{2,1,0:T(8,128)(2,1)}, u32[]{:S(2)}, u32[]{:S(2)}) %collective-permute-start.22) | collective-permute-done | bytes 1048608 | tf_op jit(solution)/shard_map/ppermute | solution.py:169
  374.0 1.5 collective-permute-start.13
  375.5 20.0 %collective-permute-done.23.refs_3_ = bf16[32,128,128]{2,1,0:T(8,128)(2,1)} collective-permute-done((bf16[32,128,128]{2,1,0:T(8,128)(2,1)}, bf16[32,128,128]{2,1,0:T(8,128)(2,1)}, u32[]{:S(2)}, u32[]{:S(2)}) %collective-permute-start.23) | collective-permute-done | bytes 1048608 | tf_op jit(solution)/shard_map/ppermute | solution.py:169
  395.5 1.9 collective-permute-start.14
  397.4 8.4 %shard_map.112.refs_4_ = f32[128,128,512]{2,1,0:T(8,128)} custom-call(f32[128,128,512]{2,1,0:T(8,128)} %latent_ref.15, bf16[512,512]{1,0:T(8,128)(2,1)S(1)} %bitcast.46, bf16[32,128,128]{2,1,0:T(8,128)(2,1)S(1)} %get-tuple-element.95.refs_0_, bf16[32,128,128]{2,1,0:T(8,128)(2,1)S(1)} %collective-permute-done.21.refs_1_, ...), custom_call_target="tpu_custom_call" | custom-call | flops 2147483648 | bytes 20971520 | tf_op jit(solution)/shard_map/pallas_call | solution.py:315
  405.8 8.2 %shard_map.113.refs_4_ = f32[128,128,512]{2,1,0:T(8,128)} custom-call(f32[128,128,512]{2,1,0:T(8,128)} %latent_ref.15, bf16[512,512]{1,0:T(8,128)(2,1)S(1)} %bitcast.47, bf16[32,128,128]{2,1,0:T(8,128)(2,1)S(1)} %get-tuple-element.91.refs_0_, bf16[32,128,128]{2,1,0:T(8,128)(2,1)S(1)} %collective-permute-done.18.refs_1_, ...), custom_call_target="tpu_custom_call", output_to_operand_aliasing={{}: (6, {})} | custom-call | flops 2147483648 | bytes 20971520 | tf_op jit(solution)/shard_map/pallas_call | solution.py:315
  413.9 4.9 collective-permute-done.16.refs_2_
  418.8 21.5 %collective-permute-done.17.refs_3_ = bf16[32,128,128]{2,1,0:T(8,128)(2,1)} collective-permute-done((bf16[32,128,128]{2,1,0:T(8,128)(2,1)S(1)}, bf16[32,128,128]{2,1,0:T(8,128)(2,1)}, u32[]{:S(2)}, u32[]{:S(2)}) %collective-permute-start.17) | collective-permute-done | bytes 1048608 | tf_op jit(solution)/shard_map/ppermute | solution.py:169
  440.3 8.2 %shard_map.114.refs_4_ = f32[128,128,512]{2,1,0:T(8,128)} custom-call(f32[128,128,512]{2,1,0:T(8,128)} %latent_ref.15, bf16[512,512]{1,0:T(8,128)(2,1)S(1)} %bitcast.48, bf16[32,128,128]{2,1,0:T(8,128)(2,1)S(1)} %get-tuple-element.87.refs_0_, bf16[32,128,128]{2,1,0:T(8,128)(2,1)S(1)} %collective-permute-done.15.refs_1_, ...), custom_call_target="tpu_custom_call", output_to_operand_aliasing={{}: (6, {})} | custom-call | flops 2147483648 | bytes 20971520 | tf_op jit(solution)/shard_map/pallas_call | solution.py:315
  448.5 1.0 copy-done.2
  449.4 14.4 %collective-permute-done.13.refs_2_ = bf16[32,128,128]{2,1,0:T(8,128)(2,1)} collective-permute-done((bf16[32,128,128]{2,1,0:T(8,128)(2,1)}, bf16[32,128,128]{2,1,0:T(8,128)(2,1)}, u32[]{:S(2)}, u32[]{:S(2)}) %collective-permute-start.13) | collective-permute-done | bytes 1048608 | tf_op jit(solution)/shard_map/ppermute | solution.py:169
  463.9 20.5 %collective-permute-done.14.refs_3_ = bf16[32,128,128]{2,1,0:T(8,128)(2,1)} collective-permute-done((bf16[32,128,128]{2,1,0:T(8,128)(2,1)}, bf16[32,128,128]{2,1,0:T(8,128)(2,1)}, u32[]{:S(2)}, u32[]{:S(2)}) %collective-permute-start.14) | collective-permute-done | bytes 1048608 | tf_op jit(solution)/shard_map/ppermute | solution.py:169
  484.4 1.3 copy-done.3
  485.7 8.4 %shard_map.115 = f32[128,128,512]{2,1,0:T(8,128)} custom-call(f32[128,128,512]{2,1,0:T(8,128)} %latent_ref.15, bf16[512,512]{1,0:T(8,128)(2,1)S(1)} %bitcast.49, bf16[32,128,128]{2,1,0:T(8,128)(2,1)S(1)} %get-tuple-element.83.refs_0_, bf16[32,128,128]{2,1,0:T(8,128)(2,1)S(1)} %copy-done.3, ...), custom_call_target="tpu_custom_call", output_to_operand_aliasing={{}: (6, {})} | custom-call | flops 2147483648 | bytes 20971520 | tf_op jit(solution)/shard_map/pallas_call | solution.py:315
  (82 shorter events, 5.0 us)
Async XLA Ops:
  6.5 1.0 copy-start
  6.5 239.3 %all-gather.5.cloned.1.call-start = ((), (), s32[]{:S(2)}) async-start(), calls=%async_computation.1 | async-start | bytes 1310720 | tf_op jit(solution)/shard_map/all_gather | solution.py:174
  14.6 1.0 copy-start.6
  15.6 21.1 %collective-permute-start = (bf16[32,128,128]{2,1,0:T(8,128)(2,1)S(1)}, bf16[32,128,128]{2,1,0:T(8,128)(2,1)S(1)}, u32[]{:S(2)}, u32[]{:S(2)}) collective-permute-start(bf16[32,128,128]{2,1,0:T(8,128)(2,1)S(1)} %get-tuple-element.53), channel_id=1, source_target_pairs={{0,4},{4,0},{8,12},{12,8},{1,5},{5,1},{9,13},{13,9},{2,6},{6,2},{1... | collective-permute-start | bytes 3145736 | tf_op jit(solution)/shard_map/ppermute | solution.py:169
  16.0 26.5 %collective-permute-start.1 = (bf16[32,128,128]{2,1,0:T(8,128)(2,1)S(1)}, bf16[32,128,128]{2,1,0:T(8,128)(2,1)S(1)}, u32[]{:S(2)}, u32[]{:S(2)}) collective-permute-start(bf16[32,128,128]{2,1,0:T(8,128)(2,1)S(1)} %get-tuple-element.54), channel_id=1, source_target_pairs={{0,8},{4,12},{8,0},{12,4},{1,9},{5,13},{9,1},{13,5},{2,10},{6,14},... | collective-permute-start | bytes 3145736 | tf_op jit(solution)/shard_map/ppermute | solution.py:169
  18.6 25.0 %copy-start.15 = (bf16[512,512]{1,0:T(8,128)(2,1)S(1)}, bf16[512,512]{1,0:T(8,128)(2,1)}, u32[]{:S(2)}) copy-start(bf16[512,512]{1,0:T(8,128)(2,1)} %param.11) | copy-start | bytes 1572868
  18.6 46.2 %collective-permute-start.2 = (bf16[32,128,128]{2,1,0:T(8,128)(2,1)}, bf16[32,128,128]{2,1,0:T(8,128)(2,1)}, u32[]{:S(2)}, u32[]{:S(2)}) collective-permute-start(bf16[32,128,128]{2,1,0:T(8,128)(2,1)} %get-tuple-element.55), channel_id=1, source_target_pairs={{0,12},{4,8},{8,4},{12,0},{1,13},{5,9},{9,5},{13,1},{2,14},{6,10},... | collective-permute-start | bytes 3145736 | tf_op jit(solution)/shard_map/ppermute | solution.py:169
  25.5 1.0 copy-start.4
  26.5 39.9 %collective-permute-start.3 = (bf16[32,128,128]{2,1,0:T(8,128)(2,1)}, bf16[32,128,128]{2,1,0:T(8,128)(2,1)}, u32[]{:S(2)}, u32[]{:S(2)}) collective-permute-start(bf16[32,128,128]{2,1,0:T(8,128)(2,1)} %get-tuple-element.58), channel_id=1, source_target_pairs={{0,4},{4,0},{8,12},{12,8},{1,5},{5,1},{9,13},{13,9},{2,6},{6,2},{1... | collective-permute-start | bytes 3145736 | tf_op jit(solution)/shard_map/ppermute | solution.py:169
  26.6 84.9 %copy-start.22 = (s32[1,16]{1,0:T(1,128)S(1)}, s32[1,16]{1,0:T(1,128)}, u32[]{:S(2)}) copy-start(s32[1,16]{1,0:T(1,128)} %param.15) | copy-start | bytes 196
  26.6 85.0 %copy-start.20 = (f32[128]{0:T(128)S(1)}, f32[128]{0:T(128)}, u32[]{:S(2)}) copy-start(f32[128]{0:T(128)} %param.13) | copy-start | bytes 1540
  26.6 61.0 %collective-permute-start.4 = (bf16[32,128,128]{2,1,0:T(8,128)(2,1)}, bf16[32,128,128]{2,1,0:T(8,128)(2,1)}, u32[]{:S(2)}, u32[]{:S(2)}) collective-permute-start(bf16[32,128,128]{2,1,0:T(8,128)(2,1)} %get-tuple-element.59), channel_id=1, source_target_pairs={{0,8},{4,12},{8,0},{12,4},{1,9},{5,13},{9,1},{13,5},{2,10},{6,14},... | collective-permute-start | bytes 3145736 | tf_op jit(solution)/shard_map/ppermute | solution.py:169
  34.7 1.0 copy-start.10
  35.7 1.0 copy-start.13
  36.7 1.0 copy-start.8
  37.7 72.0 %collective-permute-start.5 = (bf16[32,128,128]{2,1,0:T(8,128)(2,1)}, bf16[32,128,128]{2,1,0:T(8,128)(2,1)}, u32[]{:S(2)}, u32[]{:S(2)}) collective-permute-start(bf16[32,128,128]{2,1,0:T(8,128)(2,1)} %get-tuple-element.60), channel_id=1, source_target_pairs={{0,12},{4,8},{8,4},{12,0},{1,13},{5,9},{9,5},{13,1},{2,14},{6,10},... | collective-permute-start | bytes 3145736 | tf_op jit(solution)/shard_map/ppermute | solution.py:169
  42.6 1.0 copy-start.11
  43.6 67.7 %collective-permute-start.6 = (bf16[32,128,128]{2,1,0:T(8,128)(2,1)}, bf16[32,128,128]{2,1,0:T(8,128)(2,1)}, u32[]{:S(2)}, u32[]{:S(2)}) collective-permute-start(bf16[32,128,128]{2,1,0:T(8,128)(2,1)} %get-tuple-element.65), channel_id=1, source_target_pairs={{0,4},{4,0},{8,12},{12,8},{1,5},{5,1},{9,13},{13,9},{2,6},{6,2},{1... | collective-permute-start | bytes 3145736 | tf_op jit(solution)/shard_map/ppermute | solution.py:169
  45.1 66.5 %copy-start.7 = (bf16[32,128,128]{2,1,0:T(8,128)(2,1)S(1)}, bf16[32,128,128]{2,1,0:T(8,128)(2,1)}, u32[]{:S(2)}) copy-start(bf16[32,128,128]{2,1,0:T(8,128)(2,1)} %copy-done.6) | copy-start | bytes 3145732
  45.2 66.5 %copy-start.12 = (bf16[32,128,128]{2,1,0:T(8,128)(2,1)S(1)}, bf16[32,128,128]{2,1,0:T(8,128)(2,1)}, u32[]{:S(2)}) copy-start(bf16[32,128,128]{2,1,0:T(8,128)(2,1)} %copy-done.11) | copy-start | bytes 3145732
  45.2 74.8 %copy-start.5 = (bf16[32,128,128]{2,1,0:T(8,128)(2,1)S(1)}, bf16[32,128,128]{2,1,0:T(8,128)(2,1)}, u32[]{:S(2)}) copy-start(bf16[32,128,128]{2,1,0:T(8,128)(2,1)} %copy-done.4) | copy-start | bytes 3145732
  64.8 67.7 %collective-permute-start.7 = (bf16[32,128,128]{2,1,0:T(8,128)(2,1)}, bf16[32,128,128]{2,1,0:T(8,128)(2,1)S(1)}, u32[]{:S(2)}, u32[]{:S(2)}) collective-permute-start(bf16[32,128,128]{2,1,0:T(8,128)(2,1)} %copy-done.13), channel_id=1, source_target_pairs={{0,8},{4,12},{8,0},{12,4},{1,9},{5,13},{9,1},{13,5},{2,10},{6,14},... | collective-permute-start | bytes 3145736 | tf_op jit(solution)/shard_map/ppermute | solution.py:169
  66.3 88.2 %collective-permute-start.8 = (bf16[32,128,128]{2,1,0:T(8,128)(2,1)}, bf16[32,128,128]{2,1,0:T(8,128)(2,1)S(1)}, u32[]{:S(2)}, u32[]{:S(2)}) collective-permute-start(bf16[32,128,128]{2,1,0:T(8,128)(2,1)} %copy-done.10), channel_id=1, source_target_pairs={{0,12},{4,8},{8,4},{12,0},{1,13},{5,9},{9,5},{13,1},{2,14},{6,10},... | collective-permute-start | bytes 3145736 | tf_op jit(solution)/shard_map/ppermute | solution.py:169
  87.6 74.1 %collective-permute-start.9 = (bf16[32,128,128]{2,1,0:T(8,128)(2,1)}, bf16[32,128,128]{2,1,0:T(8,128)(2,1)S(1)}, u32[]{:S(2)}, u32[]{:S(2)}) collective-permute-start(bf16[32,128,128]{2,1,0:T(8,128)(2,1)} %get-tuple-element.72), channel_id=1, source_target_pairs={{0,4},{4,0},{8,12},{12,8},{1,5},{5,1},{9,13},{13,9},{2,6},{6,2},{1... | collective-permute-start | bytes 3145736 | tf_op jit(solution)/shard_map/ppermute | solution.py:169
  109.7 67.7 %collective-permute-start.10 = (bf16[32,128,128]{2,1,0:T(8,128)(2,1)}, bf16[32,128,128]{2,1,0:T(8,128)(2,1)S(1)}, u32[]{:S(2)}, u32[]{:S(2)}) collective-permute-start(bf16[32,128,128]{2,1,0:T(8,128)(2,1)} %get-tuple-element.73), channel_id=1, source_target_pairs={{0,8},{4,12},{8,0},{12,4},{1,9},{5,13},{9,1},{13,5},{2,10},{6,14},... | collective-permute-start | bytes 3145736 | tf_op jit(solution)/shard_map/ppermute | solution.py:169
  111.3 88.2 %collective-permute-start.11 = (bf16[32,128,128]{2,1,0:T(8,128)(2,1)S(1)}, bf16[32,128,128]{2,1,0:T(8,128)(2,1)S(1)}, u32[]{:S(2)}, u32[]{:S(2)}) collective-permute-start(bf16[32,128,128]{2,1,0:T(8,128)(2,1)S(1)} %get-tuple-element.74), channel_id=1, source_target_pairs={{0,12},{4,8},{8,4},{12,0},{1,13},{5,9},{9,5},{13,1},{2,14},{6,10},... | collective-permute-start | bytes 3145736 | tf_op jit(solution)/shard_map/ppermute | solution.py:169
  111.7 1.2 copy-start.9
  161.6 44.5 %copy-start.16 = (f32[1,16,8,128]{3,2,1,0:T(8,128)S(1)}, f32[1,16,8,128]{3,2,1,0:T(8,128)}, u32[]{:S(2)}) copy-start(f32[1,16,8,128]{3,2,1,0:T(8,128)} %param.19) | copy-start | bytes 196612
  161.6 44.5 %copy-start.17 = (f32[1,16,8,128]{3,2,1,0:T(8,128)S(1)}, f32[1,16,8,128]{3,2,1,0:T(8,128)}, u32[]{:S(2)}) copy-start(f32[1,16,8,128]{3,2,1,0:T(8,128)} %param.18) | copy-start | bytes 196612
  161.6 44.5 %copy-start.21 = (f32[8]{0:T(128)S(1)}, f32[8]{0:T(128)}, u32[]{:S(2)}) copy-start(f32[8]{0:T(128)} %param.14) | copy-start | bytes 100
  161.6 44.6 %copy-start.18 = (s32[1,16,128]{2,1,0:T(8,128)S(1)}, s32[1,16,128]{2,1,0:T(8,128)}, u32[]{:S(2)}) copy-start(s32[1,16,128]{2,1,0:T(8,128)} %param.17) | copy-start | bytes 24580
  161.6 44.6 %copy-start.19 = (s32[1,16,128]{2,1,0:T(8,128)S(1)}, s32[1,16,128]{2,1,0:T(8,128)}, u32[]{:S(2)}) copy-start(s32[1,16,128]{2,1,0:T(8,128)} %param.16) | copy-start | bytes 24580
  206.9 12.4 %all-to-all-start = ((f32[1,16,3,128]{3,0,2,1:T(1,128)}), f32[1,16,3,128]{3,0,2,1:T(1,128)S(1)}, u32[]{:S(2)}, u32[]{:S(2)}) async-start(f32[1,16,3,128]{3,0,2,1:T(1,128)} %pad_maximum_fusion), calls=%async_computation | async-start | bytes 49152 | tf_op jit(solution)/shard_map/all_to_all | solution.py:217
  212.9 66.0 %all-gather.7.cloned.1.call-start = ((), (), s32[]{:S(2)}) async-start(), calls=%async_computation.2 | async-start | bytes 1310720 | tf_op jit(solution)/shard_map/all_gather | solution.py:174
  302.4 2.7 collective-permute-start.15
  302.4 4.2 collective-permute-start.18
  302.9 26.0 %collective-permute-start.19 = (bf16[32,128,128]{2,1,0:T(8,128)(2,1)S(1)}, bf16[32,128,128]{2,1,0:T(8,128)(2,1)S(1)}, u32[]{:S(2)}, u32[]{:S(2)}) collective-permute-start(bf16[32,128,128]{2,1,0:T(8,128)(2,1)S(1)} %get-tuple-element.93), channel_id=1, source_target_pairs={{0,8},{4,12},{8,0},{12,4},{1,9},{5,13},{9,1},{13,5},{2,10},{6,14},... | collective-permute-start | bytes 3145736 | tf_op jit(solution)/shard_map/ppermute | solution.py:169
  304.4 46.0 %collective-permute-start.20 = (bf16[32,128,128]{2,1,0:T(8,128)(2,1)S(1)}, bf16[32,128,128]{2,1,0:T(8,128)(2,1)S(1)}, u32[]{:S(2)}, u32[]{:S(2)}) collective-permute-start(bf16[32,128,128]{2,1,0:T(8,128)(2,1)S(1)} %get-tuple-element.94), channel_id=1, source_target_pairs={{0,12},{4,8},{8,4},{12,0},{1,13},{5,9},{9,5},{13,1},{2,14},{6,10},... | collective-permute-start | bytes 3145736 | tf_op jit(solution)/shard_map/ppermute | solution.py:169
  304.4 56.7 %collective-permute-start.21 = (bf16[32,128,128]{2,1,0:T(8,128)(2,1)}, bf16[32,128,128]{2,1,0:T(8,128)(2,1)S(1)}, u32[]{:S(2)}, u32[]{:S(2)}) collective-permute-start(bf16[32,128,128]{2,1,0:T(8,128)(2,1)} %get-tuple-element.96), channel_id=1, source_target_pairs={{0,4},{4,0},{8,12},{12,8},{1,5},{5,1},{9,13},{13,9},{2,6},{6,2},{1... | collective-permute-start | bytes 3145736 | tf_op jit(solution)/shard_map/ppermute | solution.py:169
  305.1 68.9 %collective-permute-start.22 = (bf16[32,128,128]{2,1,0:T(8,128)(2,1)}, bf16[32,128,128]{2,1,0:T(8,128)(2,1)}, u32[]{:S(2)}, u32[]{:S(2)}) collective-permute-start(bf16[32,128,128]{2,1,0:T(8,128)(2,1)} %get-tuple-element.97), channel_id=1, source_target_pairs={{0,8},{4,12},{8,0},{12,4},{1,9},{5,13},{9,1},{13,5},{2,10},{6,14},... | collective-permute-start | bytes 3145736 | tf_op jit(solution)/shard_map/ppermute | solution.py:169
  306.6 88.9 %collective-permute-start.23 = (bf16[32,128,128]{2,1,0:T(8,128)(2,1)}, bf16[32,128,128]{2,1,0:T(8,128)(2,1)}, u32[]{:S(2)}, u32[]{:S(2)}) collective-permute-start(bf16[32,128,128]{2,1,0:T(8,128)(2,1)} %get-tuple-element.98), channel_id=1, source_target_pairs={{0,12},{4,8},{8,4},{12,0},{1,13},{5,9},{9,5},{13,1},{2,14},{6,10},... | collective-permute-start | bytes 3145736 | tf_op jit(solution)/shard_map/ppermute | solution.py:169
  329.0 89.9 %collective-permute-start.16 = (bf16[32,128,128]{2,1,0:T(8,128)(2,1)}, bf16[32,128,128]{2,1,0:T(8,128)(2,1)S(1)}, u32[]{:S(2)}, u32[]{:S(2)}) collective-permute-start(bf16[32,128,128]{2,1,0:T(8,128)(2,1)} %get-tuple-element.89), channel_id=1, source_target_pairs={{0,8},{4,12},{8,0},{12,4},{1,9},{5,13},{9,1},{13,5},{2,10},{6,14},... | collective-permute-start | bytes 3145736 | tf_op jit(solution)/shard_map/ppermute | solution.py:169
  350.4 89.9 %collective-permute-start.17 = (bf16[32,128,128]{2,1,0:T(8,128)(2,1)S(1)}, bf16[32,128,128]{2,1,0:T(8,128)(2,1)}, u32[]{:S(2)}, u32[]{:S(2)}) collective-permute-start(bf16[32,128,128]{2,1,0:T(8,128)(2,1)S(1)} %get-tuple-element.90), channel_id=1, source_target_pairs={{0,12},{4,8},{8,4},{12,0},{1,13},{5,9},{9,5},{13,1},{2,14},{6,10},... | collective-permute-start | bytes 3145736 | tf_op jit(solution)/shard_map/ppermute | solution.py:169
  360.1 1.0 copy-start.14
  361.1 87.4 %collective-permute-start.12 = (bf16[32,128,128]{2,1,0:T(8,128)(2,1)}, bf16[32,128,128]{2,1,0:T(8,128)(2,1)S(1)}, u32[]{:S(2)}, u32[]{:S(2)}) collective-permute-start(bf16[32,128,128]{2,1,0:T(8,128)(2,1)} %copy-done.14), channel_id=1, source_target_pairs={{0,4},{4,0},{8,12},{12,8},{1,5},{5,1},{9,13},{13,9},{2,6},{6,2},{1... | collective-permute-start | bytes 3145736 | tf_op jit(solution)/shard_map/ppermute | solution.py:169
  374.0 89.9 %collective-permute-start.13 = (bf16[32,128,128]{2,1,0:T(8,128)(2,1)}, bf16[32,128,128]{2,1,0:T(8,128)(2,1)}, u32[]{:S(2)}, u32[]{:S(2)}) collective-permute-start(bf16[32,128,128]{2,1,0:T(8,128)(2,1)} %get-tuple-element.85), channel_id=1, source_target_pairs={{0,8},{4,12},{8,0},{12,4},{1,9},{5,13},{9,1},{13,5},{2,10},{6,14},... | collective-permute-start | bytes 3145736 | tf_op jit(solution)/shard_map/ppermute | solution.py:169
  395.5 89.0 %collective-permute-start.14 = (bf16[32,128,128]{2,1,0:T(8,128)(2,1)}, bf16[32,128,128]{2,1,0:T(8,128)(2,1)}, u32[]{:S(2)}, u32[]{:S(2)}) collective-permute-start(bf16[32,128,128]{2,1,0:T(8,128)(2,1)} %get-tuple-element.86), channel_id=1, source_target_pairs={{0,12},{4,8},{8,4},{12,0},{1,13},{5,9},{9,5},{13,1},{2,14},{6,10},... | collective-permute-start | bytes 3145736 | tf_op jit(solution)/shard_map/ppermute | solution.py:169
  448.5 1.0 copy-start.2
  484.4 9.7 %copy-start.1 = (bf16[512,512]{1,0:T(8,128)(2,1)S(1)}, bf16[512,512]{1,0:T(8,128)(2,1)}, u32[]{:S(2)}) copy-start(bf16[512,512]{1,0:T(8,128)(2,1)} %param.12) | copy-start | bytes 1572868
  484.4 1.3 copy-start.3
Sparse Core Ops, SparseCore 0:
  206.2 29.2 all-gather.4
  253.5 25.3 all-gather.6

commit v2 on v1

--- a/solution.py
+++ b/solution.py
@@ -10,6 +10,7 @@
 LANES = 128
 CHUNKS = 4
 STEP = 8
+UNROLL = 16
 VMEM = 48 << 20
 
 
@@ -108,9 +109,9 @@
     split_store(dot_nt(col_ref[...], block), out_refs)
 
 
-def density_kernel(parts, chained, mean_ref, row_ref, start_ref, *refs):
+def density_kernel(parts, chained, mean_ref, voxel_row_ref, row_ref, start_ref, *refs):
     in_refs = refs[:parts]
-    running_ref, density_ref, total_ref = refs[parts + (2 if chained else 0) :]
+    density_ref, total_ref, picked_ref, table_ref = refs[parts + (1 if chained else 0) :]
     step = pl.program_id(0)
 
     @pl.when(step == 0)
@@ -124,23 +125,55 @@
         for k in range(STEP):
             density = jnp.exp(mean_ref[step * STEP + k] + field[k * LANES : (k + 1) * LANES, rows])
             total = total + density
-            running_ref[k, rows] = total
+            place = (step * STEP + k) * field.shape[1] + slab * LANES
+            table_ref[pl.ds(pl.multiple_of(place, LANES), LANES), :] = total
             density_ref[k, rows] = density.astype(density_ref.dtype)
         total_ref[rows] = total
 
-
-def adjoint_kernel(row_ref, start_ref, grad_ref, density_ref, *refs):
-    *out_refs, total_ref, field_ref = refs
-
-    @pl.when(pl.program_id(0) == 0)
+    @pl.when(step == pl.num_programs(0) - 1)
+    def _():
+        def pick(i, carry):
+            first = i * UNROLL
+            found = [
+                table_ref[pl.ds(voxel_row_ref[first + j], 1), :] for j in range(UNROLL)
+            ]
+            for j in range(UNROLL):
+                picked_ref[pl.ds(first + j, 1), :] = found[j]
+            return carry
+
+        lax.fori_loop(0, picked_ref.shape[0] // UNROLL, pick, 0)
+
+
+def adjoint_kernel(voxel_row_ref, row_ref, start_ref, value_ref, density_ref, *refs):
+    *out_refs, total_ref, field_ref, table_ref = refs
+    step = pl.program_id(0)
+    block = pl.num_programs(0) - 1 - step
+
+    @pl.when(step == 0)
     def _():
         total_ref[...] = start_ref[...]
+
+        def clear(i, carry):
+            place = pl.multiple_of(i * LANES, LANES)
+            table_ref[pl.ds(place, LANES), :] = jnp.zeros((LANES, LANES), jnp.float32)
+            return carry
+
+        lax.fori_loop(0, table_ref.shape[0] // LANES, clear, 0)
+
+        def add(i, carry):
+            for j in range(UNROLL):
+                place = pl.ds(voxel_row_ref[i * UNROLL + j], 1)
+                table_ref[place, :] = table_ref[place, :] + value_ref[pl.ds(i * UNROLL + j, 1), :]
+            return carry
+
+        lax.fori_loop(0, value_ref.shape[0] // UNROLL, add, 0)
 
     for slab in range(total_ref.shape[0] // LANES):
         rows = slice(slab * LANES, (slab + 1) * LANES)
         total = total_ref[rows]
         for k in reversed(range(STEP)):
-            total = total + grad_ref[k, rows]
+            place = (block * STEP + k) * total_ref.shape[0] + slab * LANES
+            total = total + table_ref[pl.ds(pl.multiple_of(place, LANES), LANES), :]
             field_ref[k * LANES : (k + 1) * LANES, rows] = (
                 total * density_ref[k, rows].astype(jnp.float32)
             ).astype(jnp.bfloat16)
@@ -158,7 +191,7 @@
     return pl.pallas_call(
         kernel,
         compiler_params=pltpu.CompilerParams(vmem_limit_bytes=VMEM),
-        cost_estimate=pl.CostEstimate(flops=cost[0], bytes_accessed=cost[1], transcendentals=0),
+        cost_estimate=pl.CostEstimate(flops=cost[0] // 16, bytes_accessed=cost[1] // 16, transcendentals=0),
         **kwargs,
     )
 
@@ -250,43 +283,50 @@
         )(latent, col_order)
         arrived.append(exchange(sent))
 
+    table_rows = chunk * pixel_rows
+    stars = voxel.shape[0]
+    voxel_row = [
+        jnp.clip(voxel // LANES - c * table_rows, 0, table_rows - 1) for c in range(CHUNKS)
+    ]
+    inside = [(voxel // (table_rows * LANES) == c)[:, None] for c in range(CHUNKS)]
+    scalars = pl.BlockSpec(memory_space=pltpu.SMEM)
+    table = pltpu.VMEM((table_rows, LANES), jnp.float32)
+
     kept = []
     total = jnp.zeros((pixel_rows, LANES), jnp.float32)
+    found = jnp.zeros((stars, LANES), jnp.float32)
     for c in range(CHUNKS):
-        *kept, total = call(
+        *kept, total, picked = call(
             functools.partial(density_kernel, parts, c > 0),
-            (flops, chunk * rows * cols * 8),
+            (flops, chunk * rows * cols * 4),
             grid=(steps,),
-            in_specs=[
-                pl.BlockSpec(memory_space=pltpu.SMEM),
-                whole((all_rows, all_rows)),
-                whole((pixel_rows, LANES)),
-            ]
+            in_specs=[scalars, scalars, whole((all_rows, all_rows)), whole((pixel_rows, LANES))]
             + [piece] * parts
             + [anywhere] * len(kept),
             out_specs=[
                 placed(pixel_block, c),
-                placed(pixel_block, c),
                 whole((pixel_rows, LANES)),
+                whole((stars, LANES)),
             ],
             out_shape=[
-                jax.ShapeDtypeStruct((bins, pixel_rows, LANES), jnp.float32),
                 jax.ShapeDtypeStruct((bins, pixel_rows, LANES), jnp.bfloat16),
                 jax.ShapeDtypeStruct((pixel_rows, LANES), jnp.float32),
+                jax.ShapeDtypeStruct((stars, LANES), jnp.float32),
             ],
-            input_output_aliases={3 + parts + n: n for n in range(len(kept))},
-        )(log_mean[c * chunk : (c + 1) * chunk], row_order, total, *arrived[c], *kept)
-    running, density = kept
+            scratch_shapes=[table],
+            input_output_aliases={4 + parts: 0} if c > 0 else {},
+        )(log_mean[c * chunk : (c + 1) * chunk], voxel_row[c], row_order, total, *arrived[c], *kept)
+        found = jnp.where(inside[c], picked, found)
+    density = kept[0]
 
     exact = lax.Precision.HIGHEST
     nearer = masked_sum(total, True)
-    before = jnp.sum(jnp.dot(at_row, nearer, precision=exact) * at_lane, axis=1)
-    predicted = running.reshape(-1)[voxel] + before
+    before = jnp.dot(at_row, nearer, precision=exact)
+    predicted = jnp.sum((found + before) * at_lane, axis=1)
     coeff = slope * predicted - offset
-    grad_ext = jnp.zeros((bins * block_pixels,), jnp.float32).at[voxel].add(coeff)
-    grad_ext = grad_ext.reshape(bins, pixel_rows, LANES)
+    values = at_lane * coeff[:, None]
     own = lax.dot_general(
-        at_row, at_lane * coeff[:, None], (((0,), (0,)), ((), ())), precision=exact
+        at_row, values, (((0,), (0,)), ((), ())), precision=exact
     )
     total = masked_sum(own, False)
 
@@ -294,20 +334,21 @@
     for c in reversed(range(CHUNKS)):
         *sent, total = call(
             adjoint_kernel,
-            (flops, chunk * rows * cols * 8),
+            (flops, chunk * rows * cols * 4),
             grid=(steps,),
             in_specs=[
+                scalars,
                 whole((all_rows, all_rows)),
                 whole((pixel_rows, LANES)),
-                placed(pixel_block, c, True),
+                whole((stars, LANES)),
                 placed(pixel_block, c, True),
             ],
             out_specs=[pl.BlockSpec((STEP, LANES, LANES), lambda i: (steps - 1 - i, 0, 0))]
             * parts
             + [whole((pixel_rows, LANES))],
             out_shape=pieces + [jax.ShapeDtypeStruct((pixel_rows, LANES), jnp.float32)],
-            scratch_shapes=[pltpu.VMEM((STEP * LANES, all_rows), jnp.bfloat16)],
-        )(row_turned, total, grad_ext, density)
+            scratch_shapes=[pltpu.VMEM((STEP * LANES, all_rows), jnp.bfloat16), table],
+        )(voxel_row[c], row_turned, total, jnp.where(inside[c], values, 0.0), density)
         arrived[c] = exchange(sent)
 
     out = []

time: 503 us -> 541 us (1.076)
  Pallas kernels: 118 us -> 158 us
  waiting for transfers between devices: 268 us -> 297 us
  local copies, waits for them, and re-layouts: 40 us -> 22.8 us
  other arithmetic: 28.7 us -> 14.4 us
    ppermute x24, waiting for transfers between devices: 261 us -> 165 us  [exchange(): lax.ppermute(parts[b], 'ang', [(i, i ^ b) for i in range(count)])]
    all_to_all x1, waiting for transfers between devices: 6.22 us -> 79.6 us  [fused(): lax.all_to_all(packed, ('ang', 'dist'), split_axis=1, concat_axis=0, tile...]
    all_gather x2, waiting for transfers between devices: 0.46 us -> 52.5 us  [masked_sum(): every = lax.all_gather(totals[None], 'dist', axis=0, tiled=True)]
    pallas_call x4, Pallas kernels: 29.9 us -> 66.9 us  [fused(): call(adjoint_kernel, (flops, chunk * rows * cols * 4), grid=(steps,), in_...]
    gather x1 -> x0, local copies, waits for them, and re-layouts: 26.4 us -> none  [fused(): predicted = running.reshape(-1)[voxel] + before]
    scatter-add x1 -> x0, other arithmetic: 25 us -> none  [fused(): jnp.zeros((bins * block_pixels,), jnp.float32).at[voxel].add(coeff)]
    unnamed x47 -> x73, local copies, waits for them, and re-layouts: 11.6 us -> 20.8 us
    reduce_sum x0 -> x1, other arithmetic: none -> 6.12 us  [fused(): predicted = jnp.sum((found + before) * at_lane, axis=1)]
  transfers between devices with their start and end apart: 27 -> 27, of which waited for: 18 -> 14; matrix products, arithmetic and copies ran while one was open for 11% -> 2% of each run, Pallas kernels for 15% -> 22%
where the time goes in v2:
time: 541 us; the launch traced here: 540 us
  waiting for transfers between devices  297 us (55%)
  Pallas kernels  158 us (29%)
  starting transfers between devices  26.8 us (5%)
  local copies, waits for them, and re-layouts  22.8 us (4%)
  other arithmetic  14.4 us (3%)
  between operations  13.7 us (3%)
  matrix products  6.91 us (1%)
    ppermute x24, waiting for transfers between devices, exchange(): lax.ppermute(parts[b], 'ang', [(i, i ^ b) for i in range(count)])  165 us
    all_to_all x1, waiting for transfers between devices, fused(): lax.all_to_all(packed, ('ang', 'dist'), split_axis=1, concat_axis=0, tile...  79.6 us
    pallas_call x4, Pallas kernels, fused(): call(adjoint_kernel, (flops, chunk * rows * cols * 4), grid=(steps,), in_...  66.9 us
    all_gather x2, waiting for transfers between devices, masked_sum(): every = lax.all_gather(totals[None], 'dist', axis=0, tiled=True)  52.5 us
    pallas_call x4, Pallas kernels, fused(): call(functools.partial(output_kernel, parts), (flops, chunk * rows * cols...  33.3 us
    pallas_call x4, Pallas kernels, fused(): call(functools.partial(density_kernel, parts, c > 0), (flops, chunk * row...  33 us
    pallas_call x4, Pallas kernels, fused(): call(column_kernel, (flops, chunk * rows * cols * 6), grid=(steps,), in_s...  24.6 us
    ppermute x24, starting transfers between devices, exchange(): lax.ppermute(parts[b], 'ang', [(i, i ^ b) for i in range(count)])  21.8 us
  transfers between devices with their start and end apart: 27, of which 14 were waited for; matrix products, arithmetic and copies ran while one was open for 2% of the time, Pallas kernels for 22%

profile of v2, /device:TPU:0, one launch (start us, length us, event | category | flops | bytes accessed | tf_op | source)
XLA Modules:
  0.0 539.7 jit_solution(16255604769988886738)
XLA Ops:
  6.6 1.0 copy-done
  8.2 6.6 %shard_map.104 = (bf16[32,128,128]{2,1,0:T(8,128)(2,1)S(1)}, bf16[32,128,128]{2,1,0:T(8,128)(2,1)S(1)}, bf16[32,128,128]{2,1,0:T(8,128)(2,1)}, bf16[32,128,128]{2,1,0:T(8,128)(2,1)}) custom-call(f32[128,128,512]{2,1,0:T(8,128)} %latent_ref.15, bf16[512,512]{1,0:T(8,128)(2,1)S(1)} %bitcast.54), custom_call_target="tpu_custom_call" | custom-call | flops 134217728 | bytes 786432 | tf_op jit(solution)/shard_map/pallas_call | solution.py:276
  15.2 5.6 %shard_map.102 = (bf16[32,128,128]{2,1,0:T(8,128)(2,1)S(1)}, bf16[32,128,128]{2,1,0:T(8,128)(2,1)S(1)}, bf16[32,128,128]{2,1,0:T(8,128)(2,1)S(1)}, bf16[32,128,128]{2,1,0:T(8,128)(2,1)S(1)}) custom-call(f32[128,128,512]{2,1,0:T(8,128)} %latent_ref.15, bf16[512,512]{1,0:T(8,128)(2,1)S(1)} %bitcast.55), custom_call_target="tpu_custom_call" | custom-call | flops 134217728 | bytes 786432 | tf_op jit(solution)/shard_map/pallas_call | solution.py:276
  20.8 1.0 copy-done.8
  21.8 3.0 collective-permute-start.4
  24.9 5.6 %shard_map.100 = (bf16[32,128,128]{2,1,0:T(8,128)(2,1)S(1)}, bf16[32,128,128]{2,1,0:T(8,128)(2,1)S(1)}, bf16[32,128,128]{2,1,0:T(8,128)(2,1)S(1)}, bf16[32,128,128]{2,1,0:T(8,128)(2,1)S(1)}) custom-call(f32[128,128,512]{2,1,0:T(8,128)} %latent_ref.15, bf16[512,512]{1,0:T(8,128)(2,1)S(1)} %bitcast.56), custom_call_target="tpu_custom_call" | custom-call | flops 134217728 | bytes 786432 | tf_op jit(solution)/shard_map/pallas_call | solution.py:276
  31.6 2.0 collective-permute-start.1
  33.9 14.9 %collective-permute-done.4.refs_2_ = bf16[32,128,128]{2,1,0:T(8,128)(2,1)S(1)} collective-permute-done((bf16[32,128,128]{2,1,0:T(8,128)(2,1)S(1)}, bf16[32,128,128]{2,1,0:T(8,128)(2,1)S(1)}, u32[]{:S(2)}, u32[]{:S(2)}) %collective-permute-start.4) | collective-permute-done | bytes 1048608 | tf_op jit(solution)/shard_map/ppermute | solution.py:202
  48.8 2.1 collective-permute-start.7
  50.8 20.0 %collective-permute-done.5.refs_3_ = bf16[32,128,128]{2,1,0:T(8,128)(2,1)} collective-permute-done((bf16[32,128,128]{2,1,0:T(8,128)(2,1)S(1)}, bf16[32,128,128]{2,1,0:T(8,128)(2,1)}, u32[]{:S(2)}, u32[]{:S(2)}) %collective-permute-start.5) | collective-permute-done | bytes 1048608 | tf_op jit(solution)/shard_map/ppermute | solution.py:202
  70.8 2.0 collective-permute-start.8
  72.8 6.8 %shard_map.106 = (bf16[32,128,128]{2,1,0:T(8,128)(2,1)S(1)}, bf16[32,128,128]{2,1,0:T(8,128)(2,1)}, bf16[32,128,128]{2,1,0:T(8,128)(2,1)}, bf16[32,128,128]{2,1,0:T(8,128)(2,1)}) custom-call(f32[128,128,512]{2,1,0:T(8,128)} %latent_ref.15, bf16[512,512]{1,0:T(8,128)(2,1)S(1)} %bitcast.57), custom_call_target="tpu_custom_call" | custom-call | flops 134217728 | bytes 786432 | tf_op jit(solution)/shard_map/pallas_call | solution.py:276
  79.6 1.0 copy-done.14
  80.6 1.0 copy-done.18
  81.6 12.1 %collective-permute-done.1.refs_2_ = bf16[32,128,128]{2,1,0:T(8,128)(2,1)S(1)} collective-permute-done((bf16[32,128,128]{2,1,0:T(8,128)(2,1)S(1)}, bf16[32,128,128]{2,1,0:T(8,128)(2,1)S(1)}, u32[]{:S(2)}, u32[]{:S(2)}) %collective-permute-start.1) | collective-permute-done | bytes 1048608 | tf_op jit(solution)/shard_map/ppermute | solution.py:202
  93.7 1.0 copy-done.20
  94.7 2.1 collective-permute-start.10
  96.8 19.0 %collective-permute-done.2.refs_3_ = bf16[32,128,128]{2,1,0:T(8,128)(2,1)S(1)} collective-permute-done((bf16[32,128,128]{2,1,0:T(8,128)(2,1)S(1)}, bf16[32,128,128]{2,1,0:T(8,128)(2,1)S(1)}, u32[]{:S(2)}, u32[]{:S(2)}) %collective-permute-start.2) | collective-permute-done | bytes 1048608 | tf_op jit(solution)/shard_map/ppermute | solution.py:202
  115.8 1.9 collective-permute-start.11
  118.3 5.0 all-to-all-start
  123.5 1.3 copy.53
  126.1 79.6 %all-to-all-done = f32[1,16,3,128]{3,0,2,1:T(1,128)S(1)} async-done(((f32[1,16,3,128]{3,0,2,1:T(1,128)}), f32[1,16,3,128]{3,0,2,1:T(1,128)S(1)}, u32[]{:S(2)}, u32[]{:S(2)}) %all-to-all-start) | async-done | bytes 24608 | tf_op jit(solution)/shard_map/all_to_all | solution.py:250
  205.8 1.3 copy-done.17
  207.1 1.2 copy-done.19
  208.3 1.2 copy-done.21
  209.5 7.9 %shard_map.101 = (bf16[128,512,128]{2,1,0:T(8,128)(2,1)}, f32[512,128]{1,0:T(8,128)S(1)}, f32[2048,128]{1,0:T(8,128)S(1)}) custom-call(f32[32]{0:T(128)S(1)} %get-tuple-element.117.mean_ref, s32[2048]{0:T(1024)S(1)} %get-tuple-element.107.voxel_row_ref, bf16[512,512]{1,0:T(8,128)(2,1)S(1)} %copy.59.row_ref, f32[512,128]{1,0:T(8,128)S(1)} %broadcast_in_dim.106.start_ref, ...), custom_call_target="tpu_custom_call" | custom-call | flops 134217728 | bytes 524288 | tf_op jit(solution)/shard_map/pallas_call | solution.py:299
  217.4 1.0 copy-done.22
  218.4 1.2 copy-done.9
  219.6 1.2 copy-done.11
  220.9 1.2 copy-done.13
  222.1 8.0 %shard_map.103 = (bf16[128,512,128]{2,1,0:T(8,128)(2,1)}, f32[512,128]{1,0:T(8,128)S(1)}, f32[2048,128]{1,0:T(8,128)S(1)}) custom-call(f32[32]{0:T(128)S(1)} %get-tuple-element.120.mean_ref, s32[2048]{0:T(1024)S(1)} %get-tuple-element.106.voxel_row_ref, bf16[512,512]{1,0:T(8,128)(2,1)S(1)} %copy.59.row_ref, ...), custom_call_target="tpu_custom_call", output_to_operand_aliasing={{0}: (8, {})} | custom-call | flops 134217728 | bytes 524288 | tf_op jit(solution)/shard_map/pallas_call | solution.py:299
  230.1 8.6 %shard_map.105 = (bf16[128,512,128]{2,1,0:T(8,128)(2,1)}, f32[512,128]{1,0:T(8,128)S(1)}, f32[2048,128]{1,0:T(8,128)S(1)}) custom-call(f32[32]{0:T(128)S(1)} %get-tuple-element.118.mean_ref, s32[2048]{0:T(1024)S(1)} %get-tuple-element.105.voxel_row_ref, bf16[512,512]{1,0:T(8,128)(2,1)S(1)} %copy.59.row_ref, ...), custom_call_target="tpu_custom_call", output_to_operand_aliasing={{0}: (8, {})} | custom-call | flops 134217728 | bytes 524288 | tf_op jit(solution)/shard_map/pallas_call | solution.py:299
  239.7 8.6 %shard_map.107 = (bf16[128,512,128]{2,1,0:T(8,128)(2,1)}, f32[512,128]{1,0:T(8,128)}, f32[2048,128]{1,0:T(8,128)S(1)}) custom-call(f32[32]{0:T(128)S(1)} %get-tuple-element.119.mean_ref, s32[2048]{0:T(1024)S(1)} %get-tuple-element.104.voxel_row_ref, bf16[512,512]{1,0:T(8,128)(2,1)S(1)} %copy.59.row_ref, ...), custom_call_target="tpu_custom_call", output_to_operand_aliasing={{0}: (8, {})} | custom-call | flops 134217728 | bytes 524288 | tf_op jit(solution)/shard_map/pallas_call | solution.py:299
  248.3 1.0 copy-done.26
  249.3 29.5 %all-gather.5.cloned.1.call-done = f32[2048,128]{1,0:T(8,128)} async-done(((f32[512,128]{1,0:T(8,128)}), f32[2048,128]{1,0:T(8,128)}) %all-gather.5.cloned.1.call-update) | async-done | bytes 1048592 | tf_op jit(solution)/shard_map/all_gather | solution.py:207
  278.9 1.4 select_reduce_fusion.2
  280.2 2.0 fusion.1
  282.2 6.1 %select_reduce_fusion.1 = f32[2048]{0:T(1024)S(1)} fusion(f32[2048,128]{1,0:T(8,128)S(1)} %fusion.1, f32[2048,128]{1,0:T(8,128)} %copy-done.26, f32[2048,128]{1,0:T(8,128)} %copy-done.25, f32[2048,128]{1,0:T(8,128)} %copy-done.24, f32[2048,128]{1,0:T(8,128)S(1)} %copy-done.23, s32[2048]{0:T(1024)S(1)} %get-tuple-element.108, ...), kind=kLoop, calls=%fused_computation.13 | loop fusion | flops 2095104 | bytes 5267456 | tf_op jit(solution)/shard_map/reduce_sum | solution.py:325
  288.4 5.0 fusion
  293.4 4.6 select_select_fusion
  298.0 22.9 %all-gather.7.cloned.1.call-done = f32[2048,128]{1,0:T(8,128)} async-done(((f32[512,128]{1,0:T(8,128)}), f32[2048,128]{1,0:T(8,128)}) %all-gather.7.cloned.1.call-update) | async-done | bytes 1048592 | tf_op jit(solution)/shard_map/all_gather | solution.py:207
  320.9 1.4 select_reduce_fusion.start_ref
  322.3 18.0 %shard_map.108 = (bf16[32,128,128]{2,1,0:T(8,128)(2,1)S(1)}, bf16[32,128,128]{2,1,0:T(8,128)(2,1)}, bf16[32,128,128]{2,1,0:T(8,128)(2,1)}, bf16[32,128,128]{2,1,0:T(8,128)(2,1)S(1)}, f32[512,128]{1,0:T(8,128)S(1)}) custom-call(s32[2048]{0:T(1024)S(1)} %get-tuple-element.104.voxel_row_ref, bf16[512,512]{1,0:T(8,128)(2,1)S(1)} %bitcast.63, ...), custom_call_target="tpu_custom_call" | custom-call | flops 134217728 | bytes 524288 | tf_op jit(solution)/shard_map/pallas_call | solution.py:335
  340.4 1.4 collective-permute-start.22
  342.2 15.7 %shard_map.109 = (bf16[32,128,128]{2,1,0:T(8,128)(2,1)S(1)}, bf16[32,128,128]{2,1,0:T(8,128)(2,1)}, bf16[32,128,128]{2,1,0:T(8,128)(2,1)}, bf16[32,128,128]{2,1,0:T(8,128)(2,1)}, f32[512,128]{1,0:T(8,128)S(1)}) custom-call(s32[2048]{0:T(1024)S(1)} %get-tuple-element.105.voxel_row_ref, bf16[512,512]{1,0:T(8,128)(2,1)S(1)} %bitcast.64, ...), custom_call_target="tpu_custom_call" | custom-call | flops 134217728 | bytes 524288 | tf_op jit(solution)/shard_map/pallas_call | solution.py:335
  358.3 1.2 collective-permute-start.19
  359.5 15.8 %shard_map.110 = (bf16[32,128,128]{2,1,0:T(8,128)(2,1)S(1)}, bf16[32,128,128]{2,1,0:T(8,128)(2,1)}, bf16[32,128,128]{2,1,0:T(8,128)(2,1)}, bf16[32,128,128]{2,1,0:T(8,128)(2,1)}, f32[512,128]{1,0:T(8,128)S(1)}) custom-call(s32[2048]{0:T(1024)S(1)} %get-tuple-element.106.voxel_row_ref, bf16[512,512]{1,0:T(8,128)(2,1)S(1)} %bitcast.65, ...), custom_call_target="tpu_custom_call" | custom-call | flops 134217728 | bytes 524288 | tf_op jit(solution)/shard_map/pallas_call | solution.py:335
  376.0 12.2 %collective-permute-done.23.refs_3_ = bf16[32,128,128]{2,1,0:T(8,128)(2,1)S(1)} collective-permute-done((bf16[32,128,128]{2,1,0:T(8,128)(2,1)S(1)}, bf16[32,128,128]{2,1,0:T(8,128)(2,1)S(1)}, u32[]{:S(2)}, u32[]{:S(2)}) %collective-permute-start.23) | collective-permute-done | bytes 1048608 | tf_op jit(solution)/shard_map/ppermute | solution.py:202
  388.2 1.4 collective-permute-start.16
  390.2 17.3 %shard_map.111 = (bf16[32,128,128]{2,1,0:T(8,128)(2,1)S(1)}, bf16[32,128,128]{2,1,0:T(8,128)(2,1)S(1)}, bf16[32,128,128]{2,1,0:T(8,128)(2,1)S(1)}, bf16[32,128,128]{2,1,0:T(8,128)(2,1)S(1)}, f32[512,128]{1,0:T(8,128)}) custom-call(s32[2048]{0:T(1024)S(1)} %get-tuple-element.107.voxel_row_ref, bf16[512,512]{1,0:T(8,128)(2,1)S(1)} %bitcast.66, ...), custom_call_target="tpu_custom_call" | custom-call | flops 134217728 | bytes 524288 | tf_op jit(solution)/shard_map/pallas_call | solution.py:335
  407.5 1.0 copy-done.27
  408.5 3.0 collective-permute-done.19.refs_2_
  411.5 21.8 %collective-permute-done.20.refs_3_ = bf16[32,128,128]{2,1,0:T(8,128)(2,1)} collective-permute-done((bf16[32,128,128]{2,1,0:T(8,128)(2,1)}, bf16[32,128,128]{2,1,0:T(8,128)(2,1)}, u32[]{:S(2)}, u32[]{:S(2)}) %collective-permute-start.20) | collective-permute-done | bytes 1048608 | tf_op jit(solution)/shard_map/ppermute | solution.py:202
  433.3 1.4 collective-permute-start.13
  435.2 8.2 %shard_map.112.refs_4_ = f32[128,128,512]{2,1,0:T(8,128)} custom-call(f32[128,128,512]{2,1,0:T(8,128)} %latent_ref.15, bf16[512,512]{1,0:T(8,128)(2,1)S(1)} %bitcast.58, bf16[32,128,128]{2,1,0:T(8,128)(2,1)S(1)} %get-tuple-element.95.refs_0_, bf16[32,128,128]{2,1,0:T(8,128)(2,1)S(1)} %collective-permute-done.21.refs_1_, ...), custom_call_target="tpu_custom_call" | custom-call | flops 134217728 | bytes 1310720 | tf_op jit(solution)/shard_map/pallas_call | solution.py:356
  443.4 8.2 %shard_map.113.refs_4_ = f32[128,128,512]{2,1,0:T(8,128)} custom-call(f32[128,128,512]{2,1,0:T(8,128)} %latent_ref.15, bf16[512,512]{1,0:T(8,128)(2,1)S(1)} %bitcast.59, bf16[32,128,128]{2,1,0:T(8,128)(2,1)S(1)} %get-tuple-element.91.refs_0_, bf16[32,128,128]{2,1,0:T(8,128)(2,1)S(1)} %collective-permute-done.18.refs_1_, ...), custom_call_target="tpu_custom_call", output_to_operand_aliasing={{}: (6, {})} | custom-call | flops 134217728 | bytes 1310720 | tf_op jit(solution)/shard_map/pallas_call | solution.py:356
  451.6 5.0 collective-permute-done.16.refs_2_
  456.5 21.7 %collective-permute-done.17.refs_3_ = bf16[32,128,128]{2,1,0:T(8,128)(2,1)} collective-permute-done((bf16[32,128,128]{2,1,0:T(8,128)(2,1)}, bf16[32,128,128]{2,1,0:T(8,128)(2,1)}, u32[]{:S(2)}, u32[]{:S(2)}) %collective-permute-start.17) | collective-permute-done | bytes 1048608 | tf_op jit(solution)/shard_map/ppermute | solution.py:202
  478.2 8.5 %shard_map.114.refs_4_ = f32[128,128,512]{2,1,0:T(8,128)} custom-call(f32[128,128,512]{2,1,0:T(8,128)} %latent_ref.15, bf16[512,512]{1,0:T(8,128)(2,1)S(1)} %bitcast.60, bf16[32,128,128]{2,1,0:T(8,128)(2,1)S(1)} %get-tuple-element.87.refs_0_, bf16[32,128,128]{2,1,0:T(8,128)(2,1)S(1)} %collective-permute-done.15.refs_1_, ...), custom_call_target="tpu_custom_call", output_to_operand_aliasing={{}: (6, {})} | custom-call | flops 134217728 | bytes 1310720 | tf_op jit(solution)/shard_map/pallas_call | solution.py:356
  486.7 1.0 copy-done.4
  487.7 13.8 %collective-permute-done.13.refs_2_ = bf16[32,128,128]{2,1,0:T(8,128)(2,1)} collective-permute-done((bf16[32,128,128]{2,1,0:T(8,128)(2,1)S(1)}, bf16[32,128,128]{2,1,0:T(8,128)(2,1)}, u32[]{:S(2)}, u32[]{:S(2)}) %collective-permute-start.13) | collective-permute-done | bytes 1048608 | tf_op jit(solution)/shard_map/ppermute | solution.py:202
  501.5 21.7 %collective-permute-done.14.refs_3_ = bf16[32,128,128]{2,1,0:T(8,128)(2,1)} collective-permute-done((bf16[32,128,128]{2,1,0:T(8,128)(2,1)S(1)}, bf16[32,128,128]{2,1,0:T(8,128)(2,1)}, u32[]{:S(2)}, u32[]{:S(2)}) %collective-permute-start.14) | collective-permute-done | bytes 1048608 | tf_op jit(solution)/shard_map/ppermute | solution.py:202
  523.2 1.2 copy-done.5
  524.4 8.5 %shard_map.115 = f32[128,128,512]{2,1,0:T(8,128)} custom-call(f32[128,128,512]{2,1,0:T(8,128)} %latent_ref.15, bf16[512,512]{1,0:T(8,128)(2,1)S(1)} %bitcast.61, bf16[32,128,128]{2,1,0:T(8,128)(2,1)S(1)} %copy-done.3, bf16[32,128,128]{2,1,0:T(8,128)(2,1)S(1)} %copy-done.5, ...), custom_call_target="tpu_custom_call", output_to_operand_aliasing={{}: (6, {})} | custom-call | flops 134217728 | bytes 1310720 | tf_op jit(solution)/shard_map/pallas_call | solution.py:356
  (107 shorter events, 8.4 us)
Async XLA Ops:
  6.5 1.0 copy-start
  14.7 16.9 %collective-permute-start.6 = (bf16[32,128,128]{2,1,0:T(8,128)(2,1)S(1)}, bf16[32,128,128]{2,1,0:T(8,128)(2,1)S(1)}, u32[]{:S(2)}, u32[]{:S(2)}) collective-permute-start(bf16[32,128,128]{2,1,0:T(8,128)(2,1)S(1)} %get-tuple-element.64), channel_id=1, source_target_pairs={{0,4},{4,0},{8,12},{12,8},{1,5},{5,1},{9,13},{13,9},{2,6},{6,2},{1... | collective-permute-start | bytes 3145736 | tf_op jit(solution)/shard_map/ppermute | solution.py:202
  20.8 1.0 copy-start.8
  21.8 11.8 %collective-permute-start.3 = (bf16[32,128,128]{2,1,0:T(8,128)(2,1)S(1)}, bf16[32,128,128]{2,1,0:T(8,128)(2,1)S(1)}, u32[]{:S(2)}, u32[]{:S(2)}) collective-permute-start(bf16[32,128,128]{2,1,0:T(8,128)(2,1)S(1)} %get-tuple-element.58), channel_id=1, source_target_pairs={{0,4},{4,0},{8,12},{12,8},{1,5},{5,1},{9,13},{13,9},{2,6},{6,2},{1... | collective-permute-start | bytes 3145736 | tf_op jit(solution)/shard_map/ppermute | solution.py:202
  21.8 26.9 %collective-permute-start.4 = (bf16[32,128,128]{2,1,0:T(8,128)(2,1)S(1)}, bf16[32,128,128]{2,1,0:T(8,128)(2,1)S(1)}, u32[]{:S(2)}, u32[]{:S(2)}) collective-permute-start(bf16[32,128,128]{2,1,0:T(8,128)(2,1)S(1)} %get-tuple-element.59), channel_id=1, source_target_pairs={{0,8},{4,12},{8,0},{12,4},{1,9},{5,13},{9,1},{13,5},{2,10},{6,14},... | collective-permute-start | bytes 3145736 | tf_op jit(solution)/shard_map/ppermute | solution.py:202
  24.8 8.8 %copy-start.35 = (s32[1,16]{1,0:T(1,128)S(1)}, s32[1,16]{1,0:T(1,128)}, u32[]{:S(2)}) copy-start(s32[1,16]{1,0:T(1,128)} %param.15) | copy-start | bytes 196
  24.8 8.9 %copy-start.29 = (f32[1,16,8,128]{3,2,1,0:T(8,128)S(1)}, f32[1,16,8,128]{3,2,1,0:T(8,128)}, u32[]{:S(2)}) copy-start(f32[1,16,8,128]{3,2,1,0:T(8,128)} %param.19) | copy-start | bytes 196612
  24.8 8.9 %copy-start.30 = (f32[1,16,8,128]{3,2,1,0:T(8,128)S(1)}, f32[1,16,8,128]{3,2,1,0:T(8,128)}, u32[]{:S(2)}) copy-start(f32[1,16,8,128]{3,2,1,0:T(8,128)} %param.18) | copy-start | bytes 196612
  24.8 8.9 %copy-start.34 = (f32[8]{0:T(128)S(1)}, f32[8]{0:T(128)}, u32[]{:S(2)}) copy-start(f32[8]{0:T(128)} %param.14) | copy-start | bytes 100
  24.8 46.0 %collective-permute-start.5 = (bf16[32,128,128]{2,1,0:T(8,128)(2,1)S(1)}, bf16[32,128,128]{2,1,0:T(8,128)(2,1)}, u32[]{:S(2)}, u32[]{:S(2)}) collective-permute-start(bf16[32,128,128]{2,1,0:T(8,128)(2,1)S(1)} %get-tuple-element.60), channel_id=1, source_target_pairs={{0,12},{4,8},{8,4},{12,0},{1,13},{5,9},{9,5},{13,1},{2,14},{6,10},... | collective-permute-start | bytes 3145736 | tf_op jit(solution)/shard_map/ppermute | solution.py:202
  30.5 1.0 copy-start.16
  31.5 49.1 %collective-permute-start = (bf16[32,128,128]{2,1,0:T(8,128)(2,1)S(1)}, bf16[32,128,128]{2,1,0:T(8,128)(2,1)S(1)}, u32[]{:S(2)}, u32[]{:S(2)}) collective-permute-start(bf16[32,128,128]{2,1,0:T(8,128)(2,1)S(1)} %get-tuple-element.53), channel_id=1, source_target_pairs={{0,4},{4,0},{8,12},{12,8},{1,5},{5,1},{9,13},{13,9},{2,6},{6,2},{1... | collective-permute-start | bytes 3145736 | tf_op jit(solution)/shard_map/ppermute | solution.py:202
  31.6 48.0 %copy-start.6 = (bf16[32,128,128]{2,1,0:T(8,128)(2,1)}, bf16[32,128,128]{2,1,0:T(8,128)(2,1)S(1)}, u32[]{:S(2)}) copy-start(bf16[32,128,128]{2,1,0:T(8,128)(2,1)S(1)} %collective-permute-done.6.refs_1_) | copy-start | bytes 3145732
  31.6 62.1 %collective-permute-start.1 = (bf16[32,128,128]{2,1,0:T(8,128)(2,1)S(1)}, bf16[32,128,128]{2,1,0:T(8,128)(2,1)S(1)}, u32[]{:S(2)}, u32[]{:S(2)}) collective-permute-start(bf16[32,128,128]{2,1,0:T(8,128)(2,1)S(1)} %get-tuple-element.54), channel_id=1, source_target_pairs={{0,8},{4,12},{8,0},{12,4},{1,9},{5,13},{9,1},{13,5},{2,10},{6,14},... | collective-permute-start | bytes 3145736 | tf_op jit(solution)/shard_map/ppermute | solution.py:202
  33.6 46.0 %copy-start.10 = (bf16[32,128,128]{2,1,0:T(8,128)(2,1)}, bf16[32,128,128]{2,1,0:T(8,128)(2,1)S(1)}, u32[]{:S(2)}) copy-start(bf16[32,128,128]{2,1,0:T(8,128)(2,1)S(1)} %collective-permute-done.3.refs_1_) | copy-start | bytes 3145732
  33.6 82.1 %collective-permute-start.2 = (bf16[32,128,128]{2,1,0:T(8,128)(2,1)S(1)}, bf16[32,128,128]{2,1,0:T(8,128)(2,1)S(1)}, u32[]{:S(2)}, u32[]{:S(2)}) collective-permute-start(bf16[32,128,128]{2,1,0:T(8,128)(2,1)S(1)} %get-tuple-element.55), channel_id=1, source_target_pairs={{0,12},{4,8},{8,4},{12,0},{1,13},{5,9},{9,5},{13,1},{2,14},{6,10},... | collective-permute-start | bytes 3145736 | tf_op jit(solution)/shard_map/ppermute | solution.py:202
  48.8 30.9 %copy-start.12 = (bf16[32,128,128]{2,1,0:T(8,128)(2,1)}, bf16[32,128,128]{2,1,0:T(8,128)(2,1)S(1)}, u32[]{:S(2)}) copy-start(bf16[32,128,128]{2,1,0:T(8,128)(2,1)S(1)} %collective-permute-done.4.refs_2_) | copy-start | bytes 3145732
  48.8 181.3 %collective-permute-start.7 = (bf16[32,128,128]{2,1,0:T(8,128)(2,1)}, bf16[32,128,128]{2,1,0:T(8,128)(2,1)}, u32[]{:S(2)}, u32[]{:S(2)}) collective-permute-start(bf16[32,128,128]{2,1,0:T(8,128)(2,1)} %get-tuple-element.65), channel_id=1, source_target_pairs={{0,8},{4,12},{8,0},{12,4},{1,9},{5,13},{9,1},{13,5},{2,10},{6,14},... | collective-permute-start | bytes 3145736 | tf_op jit(solution)/shard_map/ppermute | solution.py:202
  70.8 46.9 %copy-start.31 = (s32[1,16,128]{2,1,0:T(8,128)S(1)}, s32[1,16,128]{2,1,0:T(8,128)}, u32[]{:S(2)}) copy-start(s32[1,16,128]{2,1,0:T(8,128)} %param.17) | copy-start | bytes 24580
  70.8 46.9 %copy-start.32 = (s32[1,16,128]{2,1,0:T(8,128)S(1)}, s32[1,16,128]{2,1,0:T(8,128)}, u32[]{:S(2)}) copy-start(s32[1,16,128]{2,1,0:T(8,128)} %param.16) | copy-start | bytes 24580
  70.8 52.5 %copy-start.33 = (f32[128]{0:T(128)S(1)}, f32[128]{0:T(128)}, u32[]{:S(2)}) copy-start(f32[128]{0:T(128)} %param.13) | copy-start | bytes 1540
  70.8 159.2 %collective-permute-start.8 = (bf16[32,128,128]{2,1,0:T(8,128)(2,1)}, bf16[32,128,128]{2,1,0:T(8,128)(2,1)}, u32[]{:S(2)}, u32[]{:S(2)}) collective-permute-start(bf16[32,128,128]{2,1,0:T(8,128)(2,1)} %get-tuple-element.66), channel_id=1, source_target_pairs={{0,12},{4,8},{8,4},{12,0},{1,13},{5,9},{9,5},{13,1},{2,14},{6,10},... | collective-permute-start | bytes 3145736 | tf_op jit(solution)/shard_map/ppermute | solution.py:202
  79.6 1.0 copy-start.14
  80.6 1.0 copy-start.18
  81.6 158.0 %collective-permute-start.9 = (bf16[32,128,128]{2,1,0:T(8,128)(2,1)}, bf16[32,128,128]{2,1,0:T(8,128)(2,1)}, u32[]{:S(2)}, u32[]{:S(2)}) collective-permute-start(bf16[32,128,128]{2,1,0:T(8,128)(2,1)} %get-tuple-element.70), channel_id=1, source_target_pairs={{0,4},{4,0},{8,12},{12,8},{1,5},{5,1},{9,13},{13,9},{2,6},{6,2},{1... | collective-permute-start | bytes 3145736 | tf_op jit(solution)/shard_map/ppermute | solution.py:202
  93.7 1.0 copy-start.20
  94.7 144.9 %collective-permute-start.10 = (bf16[32,128,128]{2,1,0:T(8,128)(2,1)}, bf16[32,128,128]{2,1,0:T(8,128)(2,1)}, u32[]{:S(2)}, u32[]{:S(2)}) collective-permute-start(bf16[32,128,128]{2,1,0:T(8,128)(2,1)} %get-tuple-element.71), channel_id=1, source_target_pairs={{0,8},{4,12},{8,0},{12,4},{1,9},{5,13},{9,1},{13,5},{2,10},{6,14},... | collective-permute-start | bytes 3145736 | tf_op jit(solution)/shard_map/ppermute | solution.py:202
  115.8 7.5 %copy-start.28 = (bf16[32,128,128]{2,1,0:T(8,128)(2,1)}, bf16[32,128,128]{2,1,0:T(8,128)(2,1)S(1)}, u32[]{:S(2)}) copy-start(bf16[32,128,128]{2,1,0:T(8,128)(2,1)S(1)} %collective-permute-done.2.refs_3_) | copy-start | bytes 3145732
  115.8 123.9 %collective-permute-start.11 = (bf16[32,128,128]{2,1,0:T(8,128)(2,1)}, bf16[32,128,128]{2,1,0:T(8,128)(2,1)}, u32[]{:S(2)}, u32[]{:S(2)}) collective-permute-start(bf16[32,128,128]{2,1,0:T(8,128)(2,1)} %get-tuple-element.72), channel_id=1, source_target_pairs={{0,12},{4,8},{8,4},{12,0},{1,13},{5,9},{9,5},{13,1},{2,14},{6,10},... | collective-permute-start | bytes 3145736 | tf_op jit(solution)/shard_map/ppermute | solution.py:202
  118.3 87.3 %all-to-all-start = ((f32[1,16,3,128]{3,0,2,1:T(1,128)}), f32[1,16,3,128]{3,0,2,1:T(1,128)S(1)}, u32[]{:S(2)}, u32[]{:S(2)}) async-start(f32[1,16,3,128]{3,0,2,1:T(1,128)} %pad_maximum_fusion), calls=%async_computation | async-start | bytes 49152 | tf_op jit(solution)/shard_map/all_to_all | solution.py:250
  123.3 155.5 %all-gather.5.cloned.1.call-start = ((), (), s32[]{:S(2)}) async-start(), calls=%async_computation.1 | async-start | bytes 1310720 | tf_op jit(solution)/shard_map/all_gather | solution.py:207
  205.7 24.4 %copy-start.7 = (bf16[32,128,128]{2,1,0:T(8,128)(2,1)S(1)}, bf16[32,128,128]{2,1,0:T(8,128)(2,1)}, u32[]{:S(2)}) copy-start(bf16[32,128,128]{2,1,0:T(8,128)(2,1)} %copy-done.6) | copy-start | bytes 3145732
  205.8 1.3 copy-start.17
  207.1 1.2 copy-start.19
  208.3 1.2 copy-start.21
  217.4 1.0 copy-start.22
  218.4 1.2 copy-start.9
  219.6 1.2 copy-start.11
  220.9 1.2 copy-start.13
  222.1 17.6 %copy-start.15 = (bf16[32,128,128]{2,1,0:T(8,128)(2,1)S(1)}, bf16[32,128,128]{2,1,0:T(8,128)(2,1)}, u32[]{:S(2)}) copy-start(bf16[32,128,128]{2,1,0:T(8,128)(2,1)} %copy-done.14) | copy-start | bytes 3145732
  230.1 18.2 %copy-start.24 = (f32[2048,128]{1,0:T(8,128)}, f32[2048,128]{1,0:T(8,128)S(1)}, u32[]{:S(2)}) copy-start(f32[2048,128]{1,0:T(8,128)S(1)} %get-tuple-element.76) | copy-start | bytes 3145732
  238.7 1.0 copy-start.25
  239.6 42.6 %copy-start.23 = (f32[2048,128]{1,0:T(8,128)S(1)}, f32[2048,128]{1,0:T(8,128)}, u32[]{:S(2)}) copy-start(f32[2048,128]{1,0:T(8,128)} %copy-done.22) | copy-start | bytes 3145732
  248.2 1.0 copy-start.26
  249.3 71.7 %all-gather.7.cloned.1.call-start = ((), (), s32[]{:S(2)}) async-start(), calls=%async_computation.2 | async-start | bytes 1310720 | tf_op jit(solution)/shard_map/all_gather | solution.py:207
  340.4 35.0 %collective-permute-start.21 = (bf16[32,128,128]{2,1,0:T(8,128)(2,1)}, bf16[32,128,128]{2,1,0:T(8,128)(2,1)S(1)}, u32[]{:S(2)}, u32[]{:S(2)}) collective-permute-start(bf16[32,128,128]{2,1,0:T(8,128)(2,1)} %get-tuple-element.96), channel_id=1, source_target_pairs={{0,4},{4,0},{8,12},{12,8},{1,5},{5,1},{9,13},{13,9},{2,6},{6,2},{1... | collective-permute-start | bytes 3145736 | tf_op jit(solution)/shard_map/ppermute | solution.py:202
  340.4 35.2 %collective-permute-start.22 = (bf16[32,128,128]{2,1,0:T(8,128)(2,1)}, bf16[32,128,128]{2,1,0:T(8,128)(2,1)S(1)}, u32[]{:S(2)}, u32[]{:S(2)}) collective-permute-start(bf16[32,128,128]{2,1,0:T(8,128)(2,1)} %get-tuple-element.97), channel_id=1, source_target_pairs={{0,8},{4,12},{8,0},{12,4},{1,9},{5,13},{9,1},{13,5},{2,10},{6,14},... | collective-permute-start | bytes 3145736 | tf_op jit(solution)/shard_map/ppermute | solution.py:202
  341.8 46.5 %collective-permute-start.23 = (bf16[32,128,128]{2,1,0:T(8,128)(2,1)S(1)}, bf16[32,128,128]{2,1,0:T(8,128)(2,1)S(1)}, u32[]{:S(2)}, u32[]{:S(2)}) collective-permute-start(bf16[32,128,128]{2,1,0:T(8,128)(2,1)S(1)} %get-tuple-element.98), channel_id=1, source_target_pairs={{0,12},{4,8},{8,4},{12,0},{1,13},{5,9},{9,5},{13,1},{2,14},{6,10},... | collective-permute-start | bytes 3145736 | tf_op jit(solution)/shard_map/ppermute | solution.py:202
  357.9 31.7 %collective-permute-start.18 = (bf16[32,128,128]{2,1,0:T(8,128)(2,1)}, bf16[32,128,128]{2,1,0:T(8,128)(2,1)S(1)}, u32[]{:S(2)}, u32[]{:S(2)}) collective-permute-start(bf16[32,128,128]{2,1,0:T(8,128)(2,1)} %get-tuple-element.92), channel_id=1, source_target_pairs={{0,4},{4,0},{8,12},{12,8},{1,5},{5,1},{9,13},{13,9},{2,6},{6,2},{1... | collective-permute-start | bytes 3145736 | tf_op jit(solution)/shard_map/ppermute | solution.py:202
  358.3 53.2 %collective-permute-start.19 = (bf16[32,128,128]{2,1,0:T(8,128)(2,1)}, bf16[32,128,128]{2,1,0:T(8,128)(2,1)S(1)}, u32[]{:S(2)}, u32[]{:S(2)}) collective-permute-start(bf16[32,128,128]{2,1,0:T(8,128)(2,1)} %get-tuple-element.93), channel_id=1, source_target_pairs={{0,8},{4,12},{8,0},{12,4},{1,9},{5,13},{9,1},{13,5},{2,10},{6,14},... | collective-permute-start | bytes 3145736 | tf_op jit(solution)/shard_map/ppermute | solution.py:202
  375.3 57.9 %collective-permute-start.20 = (bf16[32,128,128]{2,1,0:T(8,128)(2,1)}, bf16[32,128,128]{2,1,0:T(8,128)(2,1)}, u32[]{:S(2)}, u32[]{:S(2)}) collective-permute-start(bf16[32,128,128]{2,1,0:T(8,128)(2,1)} %get-tuple-element.94), channel_id=1, source_target_pairs={{0,12},{4,8},{8,4},{12,0},{1,13},{5,9},{9,5},{13,1},{2,14},{6,10},... | collective-permute-start | bytes 3145736 | tf_op jit(solution)/shard_map/ppermute | solution.py:202
  375.6 59.1 %collective-permute-start.15 = (bf16[32,128,128]{2,1,0:T(8,128)(2,1)}, bf16[32,128,128]{2,1,0:T(8,128)(2,1)S(1)}, u32[]{:S(2)}, u32[]{:S(2)}) collective-permute-start(bf16[32,128,128]{2,1,0:T(8,128)(2,1)} %get-tuple-element.88), channel_id=1, source_target_pairs={{0,4},{4,0},{8,12},{12,8},{1,5},{5,1},{9,13},{13,9},{2,6},{6,2},{1... | collective-permute-start | bytes 3145736 | tf_op jit(solution)/shard_map/ppermute | solution.py:202
  388.2 68.3 %collective-permute-start.16 = (bf16[32,128,128]{2,1,0:T(8,128)(2,1)}, bf16[32,128,128]{2,1,0:T(8,128)(2,1)}, u32[]{:S(2)}, u32[]{:S(2)}) collective-permute-start(bf16[32,128,128]{2,1,0:T(8,128)(2,1)} %get-tuple-element.89), channel_id=1, source_target_pairs={{0,8},{4,12},{8,0},{12,4},{1,9},{5,13},{9,1},{13,5},{2,10},{6,14},... | collective-permute-start | bytes 3145736 | tf_op jit(solution)/shard_map/ppermute | solution.py:202
  389.6 88.6 %collective-permute-start.17 = (bf16[32,128,128]{2,1,0:T(8,128)(2,1)}, bf16[32,128,128]{2,1,0:T(8,128)(2,1)}, u32[]{:S(2)}, u32[]{:S(2)}) collective-permute-start(bf16[32,128,128]{2,1,0:T(8,128)(2,1)} %get-tuple-element.90), channel_id=1, source_target_pairs={{0,12},{4,8},{8,4},{12,0},{1,13},{5,9},{9,5},{13,1},{2,14},{6,10},... | collective-permute-start | bytes 3145736 | tf_op jit(solution)/shard_map/ppermute | solution.py:202
  407.5 1.0 copy-start.27
  408.5 34.9 %copy-start.2 = (bf16[32,128,128]{2,1,0:T(8,128)(2,1)}, bf16[32,128,128]{2,1,0:T(8,128)(2,1)S(1)}, u32[]{:S(2)}) copy-start(bf16[32,128,128]{2,1,0:T(8,128)(2,1)S(1)} %get-tuple-element.83.refs_0_) | copy-start | bytes 3145732
  411.5 75.2 %collective-permute-start.12 = (bf16[32,128,128]{2,1,0:T(8,128)(2,1)}, bf16[32,128,128]{2,1,0:T(8,128)(2,1)S(1)}, u32[]{:S(2)}, u32[]{:S(2)}) collective-permute-start(bf16[32,128,128]{2,1,0:T(8,128)(2,1)} %copy-done.27), channel_id=1, source_target_pairs={{0,4},{4,0},{8,12},{12,8},{1,5},{5,1},{9,13},{13,9},{2,6},{6,2},{1... | collective-permute-start | bytes 3145736 | tf_op jit(solution)/shard_map/ppermute | solution.py:202
  433.3 68.2 %collective-permute-start.13 = (bf16[32,128,128]{2,1,0:T(8,128)(2,1)S(1)}, bf16[32,128,128]{2,1,0:T(8,128)(2,1)}, u32[]{:S(2)}, u32[]{:S(2)}) collective-permute-start(bf16[32,128,128]{2,1,0:T(8,128)(2,1)S(1)} %get-tuple-element.85), channel_id=1, source_target_pairs={{0,8},{4,12},{8,0},{12,4},{1,9},{5,13},{9,1},{13,5},{2,10},{6,14},... | collective-permute-start | bytes 3145736 | tf_op jit(solution)/shard_map/ppermute | solution.py:202
  434.7 88.5 %collective-permute-start.14 = (bf16[32,128,128]{2,1,0:T(8,128)(2,1)S(1)}, bf16[32,128,128]{2,1,0:T(8,128)(2,1)}, u32[]{:S(2)}, u32[]{:S(2)}) collective-permute-start(bf16[32,128,128]{2,1,0:T(8,128)(2,1)S(1)} %get-tuple-element.86), channel_id=1, source_target_pairs={{0,12},{4,8},{8,4},{12,0},{1,13},{5,9},{9,5},{13,1},{2,14},{6,10},... | collective-permute-start | bytes 3145736 | tf_op jit(solution)/shard_map/ppermute | solution.py:202
  478.2 44.9 %copy-start.3 = (bf16[32,128,128]{2,1,0:T(8,128)(2,1)S(1)}, bf16[32,128,128]{2,1,0:T(8,128)(2,1)}, u32[]{:S(2)}) copy-start(bf16[32,128,128]{2,1,0:T(8,128)(2,1)} %copy-done.2) | copy-start | bytes 3145732
  486.7 1.0 copy-start.4
  523.2 1.2 copy-start.5
  524.4 8.5 %copy-start.1 = (bf16[512,512]{1,0:T(8,128)(2,1)S(1)}, bf16[512,512]{1,0:T(8,128)(2,1)}, u32[]{:S(2)}) copy-start(bf16[512,512]{1,0:T(8,128)(2,1)} %param.12) | copy-start | bytes 1572868
Sparse Core Ops, SparseCore 0:
  249.4 29.4 all-gather.4
  293.5 27.4 all-gather.6

commit v3 on v2

--- a/solution.py
+++ b/solution.py
@@ -104,7 +104,7 @@
     return jnp.concatenate([ref[...].reshape(-1, LANES) for ref in refs], axis=1)
 
 
-def column_kernel(latent_ref, col_ref, *out_refs):
+def column_kernel(latent_ref, col_ref, packed_ref, *out_refs):
     block = latent_ref[...].astype(jnp.bfloat16).reshape(-1, latent_ref.shape[2])
     split_store(dot_nt(col_ref[...], block), out_refs)
 
@@ -203,16 +203,20 @@
     ]
 
 
-def masked_sum(totals, nearer):
-    every = lax.all_gather(totals[None], "dist", axis=0, tiled=True)
-    position = jnp.arange(every.shape[0], dtype=jnp.int32)
-    me = lax.axis_index("dist")
-    keep = position < me if nearer else position > me
-    return jnp.sum(jnp.where(keep[:, None, None], every, 0.0), axis=0)
+def other_sum(totals, count, nearer):
+    sums, others = totals, jnp.zeros_like(totals)
+    shift = 1
+    while shift < count:
+        pairs = [(i, i + shift) for i in range(count - shift)]
+        moved = lax.ppermute(sums, "dist", pairs if nearer else [(j, i) for i, j in pairs])
+        sums, others = sums + moved, others + moved
+        shift *= 2
+    return others
 
 
 def fused(
     parts,
+    dists,
     latent,
     row_factor,
     col_factor,
@@ -277,10 +281,10 @@
             column_kernel,
             (flops, chunk * rows * cols * 6),
             grid=(steps,),
-            in_specs=[placed(latent_block, c), whole((cols, cols))],
+            in_specs=[placed(latent_block, c), whole((cols, cols)), anywhere],
             out_specs=[piece] * parts,
             out_shape=pieces,
-        )(latent, col_order)
+        )(latent, col_order, packed)
         arrived.append(exchange(sent))
 
     table_rows = chunk * pixel_rows
@@ -320,7 +324,7 @@
     density = kept[0]
 
     exact = lax.Precision.HIGHEST
-    nearer = masked_sum(total, True)
+    nearer = other_sum(total, dists, True)
     before = jnp.dot(at_row, nearer, precision=exact)
     predicted = jnp.sum((found + before) * at_lane, axis=1)
     coeff = slope * predicted - offset
@@ -328,7 +332,7 @@
     own = lax.dot_general(
         at_row, values, (((0,), (0,)), ((), ())), precision=exact
     )
-    total = masked_sum(own, False)
+    total = other_sum(own, dists, False)
 
     arrived = [None] * CHUNKS
     for c in reversed(range(CHUNKS)):
@@ -367,11 +371,11 @@
     return out[0]
 
 
-def per_device(parts, latent, *others):
+def per_device(parts, dists, latent, *others):
     bins, rows, cols = latent.shape
     tiles = rows == LANES and cols == parts * LANES and bins % (CHUNKS * STEP) == 0
     if tiles and parts & (parts - 1) == 0 and bins * rows * cols <= 1 << 24:
-        return fused(parts, latent, *others)
+        return fused(parts, dists, latent, *others)
     return general(latent, *others)
 
 
@@ -390,5 +394,6 @@
     )
     out_specs = P(("chain", "dist"), "ang", None)
     return jax.shard_map(
-        functools.partial(per_device, mesh.shape["ang"]), mesh=mesh, in_specs=in_specs, out_specs=out_specs, check_vma=False
-    )
+        functools.partial(per_device, mesh.shape["ang"], mesh.shape["dist"]),
+        mesh=mesh, in_specs=in_specs, out_specs=out_specs, check_vma=False
+    )

time: 541 us -> 488 us (0.902)
  waiting for transfers between devices: 297 us -> 261 us
  between operations: 13.7 us -> 0.29 us
  starting transfers between devices: 26.8 us -> 34.5 us
  other arithmetic: 14.4 us -> 8.04 us
  local copies, waits for them, and re-layouts: 22.8 us -> 16.8 us
    all_to_all x1, waiting for transfers between devices: 79.6 us -> 5.84 us  [fused(): lax.all_to_all(packed, ('ang', 'dist'), split_axis=1, concat_axis=0, tile...]
    ppermute x24, waiting for transfers between devices: 165 us -> 223 us  [exchange(): lax.ppermute(parts[b], 'ang', [(i, i ^ b) for i in range(count)])]
    all_gather x2 -> x0, waiting for transfers between devices: 52.5 us -> none  [masked_sum(): every = lax.all_gather(totals[None], 'dist', axis=0, tiled=True)]
    ppermute x0 -> x4, waiting for transfers between devices: none -> 33 us  [other_sum(): lax.ppermute(sums, 'dist', pairs if nearer else [(j, i) for i, j in pairs])]
    ppermute x0 -> x4, starting transfers between devices: none -> 9.87 us  [other_sum(): lax.ppermute(sums, 'dist', pairs if nearer else [(j, i) for i, j in pairs])]
    reduce_sum x3 -> x0, other arithmetic: 8.9 us -> none  [the longest x1 6.12 us: fused(): predicted = jnp.sum((found + before) * at_lane, axis=1)]
    unnamed x73 -> x49, local copies, waits for them, and re-layouts: 20.8 us -> 14.8 us
  transfers between devices with their start and end apart: 27 -> 29, of which waited for: 14 -> 19; matrix products, arithmetic and copies ran while one was open for 2% -> 1% of each run, Pallas kernels for 22% -> 24%
where the time goes in v3:
time: 488 us; the launch traced here: 487 us
  waiting for transfers between devices  261 us (53%)
  Pallas kernels  158 us (32%)
  starting transfers between devices  34.5 us (7%)
  local copies, waits for them, and re-layouts  16.8 us (3%)
  other arithmetic  8.04 us (2%)
  matrix products  7.93 us (2%)
    ppermute x24, waiting for transfers between devices, exchange(): lax.ppermute(parts[b], 'ang', [(i, i ^ b) for i in range(count)])  223 us
    pallas_call x4, Pallas kernels, fused(): call(adjoint_kernel, (flops, chunk * rows * cols * 4), grid=(steps,), in_...  67.1 us
    pallas_call x4, Pallas kernels, fused(): call(functools.partial(output_kernel, parts), (flops, chunk * rows * cols...  33.3 us
    ppermute x4, waiting for transfers between devices, other_sum(): lax.ppermute(sums, 'dist', pairs if nearer else [(j, i) for i, j in pairs])  33 us
    pallas_call x4, Pallas kernels, fused(): call(functools.partial(density_kernel, parts, c > 0), (flops, chunk * row...  32.5 us
    pallas_call x4, Pallas kernels, fused(): call(column_kernel, (flops, chunk * rows * cols * 6), grid=(steps,), in_s...  24.6 us
    ppermute x24, starting transfers between devices, exchange(): lax.ppermute(parts[b], 'ang', [(i, i ^ b) for i in range(count)])  17.3 us
    unnamed x49, local copies, waits for them, and re-layouts  14.8 us
  transfers between devices with their start and end apart: 29, of which 19 were waited for; matrix products, arithmetic and copies ran while one was open for 1% of the time, Pallas kernels for 24%

profile of v3, /device:TPU:0, one launch (start us, length us, event | category | flops | bytes accessed | tf_op | source)
XLA Modules:
  0.0 486.5 jit_solution(73444494228515556)
XLA Ops:
  1.5 1.0 multiply_reduce_fusion.1
  3.2 7.4 %all-to-all-start = ((f32[1,16,3,128]{3,0,2,1:T(1,128)}), f32[1,16,3,128]{3,0,2,1:T(1,128)S(1)}, u32[]{:S(2)}, u32[]{:S(2)}) async-start(f32[1,16,3,128]{3,0,2,1:T(1,128)} %pad_maximum_fusion), calls=%async_computation | async-start | bytes 49152 | tf_op jit(solution)/shard_map/all_to_all | solution.py:254
  11.2 5.8 %all-to-all-done = f32[1,16,3,128]{3,0,2,1:T(1,128)S(1)} async-done(((f32[1,16,3,128]{3,0,2,1:T(1,128)}), f32[1,16,3,128]{3,0,2,1:T(1,128)S(1)}, u32[]{:S(2)}, u32[]{:S(2)}) %all-to-all-start) | async-done | bytes 24608 | tf_op jit(solution)/shard_map/all_to_all | solution.py:254
  17.0 6.6 %shard_map.104 = (bf16[32,128,128]{2,1,0:T(8,128)(2,1)S(1)}, bf16[32,128,128]{2,1,0:T(8,128)(2,1)S(1)}, bf16[32,128,128]{2,1,0:T(8,128)(2,1)}, bf16[32,128,128]{2,1,0:T(8,128)(2,1)}) custom-call(f32[128,128,512]{2,1,0:T(8,128)} %latent_ref.15, bf16[512,512]{1,0:T(8,128)(2,1)S(1)} %bitcast.51, f32[16,3,128]{2,1,0:T(4,128)S(1)} %copy.48.packed_ref), custom_call_target="tpu_custom_call" | custom-call | flops 134217728 | bytes 786432 | tf_op jit(solution)/shard_map/pallas_call | solution.py:280
  23.8 5.6 %shard_map.102 = (bf16[32,128,128]{2,1,0:T(8,128)(2,1)S(1)}, bf16[32,128,128]{2,1,0:T(8,128)(2,1)S(1)}, bf16[32,128,128]{2,1,0:T(8,128)(2,1)S(1)}, bf16[32,128,128]{2,1,0:T(8,128)(2,1)S(1)}) custom-call(f32[128,128,512]{2,1,0:T(8,128)} %latent_ref.15, bf16[512,512]{1,0:T(8,128)(2,1)S(1)} %bitcast.52, f32[16,3,128]{2,1,0:T(4,128)S(1)} %copy.48.packed_ref), custom_call_target="tpu_custom_call" | custom-call | flops 134217728 | bytes 786432 | tf_op jit(solution)/shard_map/pallas_call | solution.py:280
  29.4 1.0 copy-done.8
  32.2 5.6 %shard_map.100 = (bf16[32,128,128]{2,1,0:T(8,128)(2,1)S(1)}, bf16[32,128,128]{2,1,0:T(8,128)(2,1)S(1)}, bf16[32,128,128]{2,1,0:T(8,128)(2,1)S(1)}, bf16[32,128,128]{2,1,0:T(8,128)(2,1)S(1)}) custom-call(f32[128,128,512]{2,1,0:T(8,128)} %latent_ref.15, bf16[512,512]{1,0:T(8,128)(2,1)S(1)} %bitcast.53, f32[16,3,128]{2,1,0:T(4,128)S(1)} %copy.48.packed_ref), custom_call_target="tpu_custom_call" | custom-call | flops 134217728 | bytes 786432 | tf_op jit(solution)/shard_map/pallas_call | solution.py:280
  37.9 1.0 copy-done.16
  40.9 15.8 %collective-permute-done.4.refs_2_ = bf16[32,128,128]{2,1,0:T(8,128)(2,1)S(1)} collective-permute-done((bf16[32,128,128]{2,1,0:T(8,128)(2,1)S(1)}, bf16[32,128,128]{2,1,0:T(8,128)(2,1)S(1)}, u32[]{:S(2)}, u32[]{:S(2)}) %collective-permute-start.4) | collective-permute-done | bytes 1048608 | tf_op jit(solution)/shard_map/ppermute | solution.py:202
  57.4 20.3 %collective-permute-done.5.refs_3_ = bf16[32,128,128]{2,1,0:T(8,128)(2,1)} collective-permute-done((bf16[32,128,128]{2,1,0:T(8,128)(2,1)S(1)}, bf16[32,128,128]{2,1,0:T(8,128)(2,1)}, u32[]{:S(2)}, u32[]{:S(2)}) %collective-permute-start.5) | collective-permute-done | bytes 1048608 | tf_op jit(solution)/shard_map/ppermute | solution.py:202
  77.7 1.7 collective-permute-start.8
  79.4 6.8 %shard_map.106 = (bf16[32,128,128]{2,1,0:T(8,128)(2,1)S(1)}, bf16[32,128,128]{2,1,0:T(8,128)(2,1)}, bf16[32,128,128]{2,1,0:T(8,128)(2,1)}, bf16[32,128,128]{2,1,0:T(8,128)(2,1)}) custom-call(f32[128,128,512]{2,1,0:T(8,128)} %latent_ref.15, bf16[512,512]{1,0:T(8,128)(2,1)S(1)} %bitcast.54, f32[16,3,128]{2,1,0:T(4,128)S(1)} %copy.48.packed_ref), custom_call_target="tpu_custom_call" | custom-call | flops 134217728 | bytes 786432 | tf_op jit(solution)/shard_map/pallas_call | solution.py:280
  86.2 1.0 copy-done.14
  87.2 1.0 copy-done.18
  88.2 13.5 %collective-permute-done.1.refs_2_ = bf16[32,128,128]{2,1,0:T(8,128)(2,1)S(1)} collective-permute-done((bf16[32,128,128]{2,1,0:T(8,128)(2,1)S(1)}, bf16[32,128,128]{2,1,0:T(8,128)(2,1)S(1)}, u32[]{:S(2)}, u32[]{:S(2)}) %collective-permute-start.1) | collective-permute-done | bytes 1048608 | tf_op jit(solution)/shard_map/ppermute | solution.py:202
  101.7 1.0 copy-done.20
  103.3 19.3 %collective-permute-done.2.refs_3_ = bf16[32,128,128]{2,1,0:T(8,128)(2,1)} collective-permute-done((bf16[32,128,128]{2,1,0:T(8,128)(2,1)S(1)}, bf16[32,128,128]{2,1,0:T(8,128)(2,1)}, u32[]{:S(2)}, u32[]{:S(2)}) %collective-permute-start.2) | collective-permute-done | bytes 1048608 | tf_op jit(solution)/shard_map/ppermute | solution.py:202
  122.6 1.7 collective-permute-start.11
  126.1 1.3 copy-done.17
  127.4 1.2 copy-done.19
  128.7 1.2 copy-done.21
  129.9 7.9 %shard_map.101 = (bf16[128,512,128]{2,1,0:T(8,128)(2,1)}, f32[512,128]{1,0:T(8,128)S(1)}, f32[2048,128]{1,0:T(8,128)S(1)}) custom-call(f32[32]{0:T(128)S(1)} %get-tuple-element.117.mean_ref, s32[2048]{0:T(1024)S(1)} %get-tuple-element.107.voxel_row_ref, bf16[512,512]{1,0:T(8,128)(2,1)S(1)} %copy.55.row_ref, f32[512,128]{1,0:T(8,128)S(1)} %broadcast_in_dim.79.start_ref, ...), custom_call_target="tpu_custom_call" | custom-call | flops 134217728 | bytes 524288 | tf_op jit(solution)/shard_map/pallas_call | solution.py:303
  137.8 1.2 copy-done.9
  139.0 1.2 copy-done.11
  140.2 1.2 copy-done.13
  141.4 8.0 %shard_map.103 = (bf16[128,512,128]{2,1,0:T(8,128)(2,1)}, f32[512,128]{1,0:T(8,128)S(1)}, f32[2048,128]{1,0:T(8,128)S(1)}) custom-call(f32[32]{0:T(128)S(1)} %get-tuple-element.120.mean_ref, s32[2048]{0:T(1024)S(1)} %get-tuple-element.106.voxel_row_ref, bf16[512,512]{1,0:T(8,128)(2,1)S(1)} %copy.55.row_ref, ...), custom_call_target="tpu_custom_call", output_to_operand_aliasing={{0}: (8, {})} | custom-call | flops 134217728 | bytes 524288 | tf_op jit(solution)/shard_map/pallas_call | solution.py:303
  149.4 18.1 %collective-permute-done.8.refs_3_ = bf16[32,128,128]{2,1,0:T(8,128)(2,1)} collective-permute-done((bf16[32,128,128]{2,1,0:T(8,128)(2,1)}, bf16[32,128,128]{2,1,0:T(8,128)(2,1)}, u32[]{:S(2)}, u32[]{:S(2)}) %collective-permute-start.8) | collective-permute-done | bytes 1048608 | tf_op jit(solution)/shard_map/ppermute | solution.py:202
  167.6 8.2 %shard_map.105 = (bf16[128,512,128]{2,1,0:T(8,128)(2,1)}, f32[512,128]{1,0:T(8,128)S(1)}, f32[2048,128]{1,0:T(8,128)S(1)}) custom-call(f32[32]{0:T(128)S(1)} %get-tuple-element.118.mean_ref, s32[2048]{0:T(1024)S(1)} %get-tuple-element.105.voxel_row_ref, bf16[512,512]{1,0:T(8,128)(2,1)S(1)} %copy.55.row_ref, ...), custom_call_target="tpu_custom_call", output_to_operand_aliasing={{0}: (8, {})} | custom-call | flops 134217728 | bytes 524288 | tf_op jit(solution)/shard_map/pallas_call | solution.py:303
  175.8 15.9 %collective-permute-done.10.refs_2_ = bf16[32,128,128]{2,1,0:T(8,128)(2,1)} collective-permute-done((bf16[32,128,128]{2,1,0:T(8,128)(2,1)}, bf16[32,128,128]{2,1,0:T(8,128)(2,1)}, u32[]{:S(2)}, u32[]{:S(2)}) %collective-permute-start.10) | collective-permute-done | bytes 1048608 | tf_op jit(solution)/shard_map/ppermute | solution.py:202
  191.7 20.8 %collective-permute-done.11.refs_3_ = bf16[32,128,128]{2,1,0:T(8,128)(2,1)} collective-permute-done((bf16[32,128,128]{2,1,0:T(8,128)(2,1)}, bf16[32,128,128]{2,1,0:T(8,128)(2,1)}, u32[]{:S(2)}, u32[]{:S(2)}) %collective-permute-start.11) | collective-permute-done | bytes 1048608 | tf_op jit(solution)/shard_map/ppermute | solution.py:202
  212.5 8.4 %shard_map.107 = (bf16[128,512,128]{2,1,0:T(8,128)(2,1)}, f32[512,128]{1,0:T(8,128)S(1)}, f32[2048,128]{1,0:T(8,128)S(1)}) custom-call(f32[32]{0:T(128)S(1)} %get-tuple-element.119.mean_ref, s32[2048]{0:T(1024)S(1)} %get-tuple-element.104.voxel_row_ref, bf16[512,512]{1,0:T(8,128)(2,1)S(1)} %copy.55.row_ref, ...), custom_call_target="tpu_custom_call", output_to_operand_aliasing={{0}: (8, {})} | custom-call | flops 134217728 | bytes 524288 | tf_op jit(solution)/shard_map/pallas_call | solution.py:303
  220.9 2.4 collective-permute-start.12
  223.3 6.4 %collective-permute-done.12 = f32[512,128]{1,0:T(8,128)S(1)} collective-permute-done((f32[512,128]{1,0:T(8,128)S(1)}, f32[512,128]{1,0:T(8,128)S(1)}, u32[]{:S(2)}, u32[]{:S(2)}) %collective-permute-start.12) | collective-permute-done | bytes 262176 | tf_op jit(solution)/shard_map/ppermute | solution.py:211
  229.7 4.7 collective-permute-start.13
  234.4 5.4 %collective-permute-done.13 = f32[512,128]{1,0:T(8,128)S(1)} collective-permute-done((f32[512,128]{1,0:T(8,128)S(1)}, f32[512,128]{1,0:T(8,128)S(1)}, u32[]{:S(2)}, u32[]{:S(2)}) %collective-permute-start.13) | collective-permute-done | bytes 262176 | tf_op jit(solution)/shard_map/ppermute | solution.py:211
  239.8 3.7 select_reduce_fusion
  243.5 4.2 fusion
  247.7 1.3 collective-permute-start.14
  249.0 12.4 %collective-permute-done.14 = f32[512,128]{1,0:T(8,128)S(1)} collective-permute-done((f32[512,128]{1,0:T(8,128)S(1)}, f32[512,128]{1,0:T(8,128)S(1)}, u32[]{:S(2)}, u32[]{:S(2)}) %collective-permute-start.14) | collective-permute-done | bytes 262176 | tf_op jit(solution)/shard_map/ppermute | solution.py:211
  261.4 1.5 collective-permute-start.15
  262.9 4.7 select_select_fusion
  267.7 8.8 %collective-permute-done.15 = f32[512,128]{1,0:T(8,128)S(1)} collective-permute-done((f32[512,128]{1,0:T(8,128)S(1)}, f32[512,128]{1,0:T(8,128)S(1)}, u32[]{:S(2)}, u32[]{:S(2)}) %collective-permute-start.15) | collective-permute-done | bytes 262176 | tf_op jit(solution)/shard_map/ppermute | solution.py:211
  276.6 17.7 %shard_map.108 = (bf16[32,128,128]{2,1,0:T(8,128)(2,1)S(1)}, bf16[32,128,128]{2,1,0:T(8,128)(2,1)}, bf16[32,128,128]{2,1,0:T(8,128)(2,1)S(1)}, bf16[32,128,128]{2,1,0:T(8,128)(2,1)S(1)}, f32[512,128]{1,0:T(8,128)S(1)}) custom-call(s32[2048]{0:T(1024)S(1)} %get-tuple-element.104.voxel_row_ref, bf16[512,512]{1,0:T(8,128)(2,1)S(1)} %bitcast.60, ...), custom_call_target="tpu_custom_call" | custom-call | flops 134217728 | bytes 524288 | tf_op jit(solution)/shard_map/pallas_call | solution.py:339
  294.2 0.9 collective-permute-start.26
  295.1 1.0 collective-permute-start.27
  296.1 15.7 %shard_map.109 = (bf16[32,128,128]{2,1,0:T(8,128)(2,1)S(1)}, bf16[32,128,128]{2,1,0:T(8,128)(2,1)}, bf16[32,128,128]{2,1,0:T(8,128)(2,1)}, bf16[32,128,128]{2,1,0:T(8,128)(2,1)}, f32[512,128]{1,0:T(8,128)S(1)}) custom-call(s32[2048]{0:T(1024)S(1)} %get-tuple-element.105.voxel_row_ref, bf16[512,512]{1,0:T(8,128)(2,1)S(1)} %bitcast.61, ...), custom_call_target="tpu_custom_call" | custom-call | flops 134217728 | bytes 524288 | tf_op jit(solution)/shard_map/pallas_call | solution.py:339
  312.8 15.8 %shard_map.110 = (bf16[32,128,128]{2,1,0:T(8,128)(2,1)S(1)}, bf16[32,128,128]{2,1,0:T(8,128)(2,1)}, bf16[32,128,128]{2,1,0:T(8,128)(2,1)}, bf16[32,128,128]{2,1,0:T(8,128)(2,1)}, f32[512,128]{1,0:T(8,128)S(1)}) custom-call(s32[2048]{0:T(1024)S(1)} %get-tuple-element.106.voxel_row_ref, bf16[512,512]{1,0:T(8,128)(2,1)S(1)} %bitcast.62, ...), custom_call_target="tpu_custom_call" | custom-call | flops 134217728 | bytes 524288 | tf_op jit(solution)/shard_map/pallas_call | solution.py:339
  329.4 0.9 collective-permute-start.19
  330.3 11.6 %collective-permute-done.27.refs_3_ = bf16[32,128,128]{2,1,0:T(8,128)(2,1)S(1)} collective-permute-done((bf16[32,128,128]{2,1,0:T(8,128)(2,1)S(1)}, bf16[32,128,128]{2,1,0:T(8,128)(2,1)S(1)}, u32[]{:S(2)}, u32[]{:S(2)}) %collective-permute-start.27) | collective-permute-done | bytes 1048608 | tf_op jit(solution)/shard_map/ppermute | solution.py:202
  342.8 1.1 collective-permute-start.21
  343.8 18.0 %shard_map.111 = (bf16[32,128,128]{2,1,0:T(8,128)(2,1)S(1)}, bf16[32,128,128]{2,1,0:T(8,128)(2,1)}, bf16[32,128,128]{2,1,0:T(8,128)(2,1)}, bf16[32,128,128]{2,1,0:T(8,128)(2,1)}, f32[512,128]{1,0:T(8,128)}) custom-call(s32[2048]{0:T(1024)S(1)} %get-tuple-element.107.voxel_row_ref, bf16[512,512]{1,0:T(8,128)(2,1)S(1)} %bitcast.63, ...), custom_call_target="tpu_custom_call" | custom-call | flops 134217728 | bytes 524288 | tf_op jit(solution)/shard_map/pallas_call | solution.py:339
  361.8 3.3 collective-permute-done.23.refs_2_
  365.1 21.8 %collective-permute-done.24.refs_3_ = bf16[32,128,128]{2,1,0:T(8,128)(2,1)} collective-permute-done((bf16[32,128,128]{2,1,0:T(8,128)(2,1)}, bf16[32,128,128]{2,1,0:T(8,128)(2,1)}, u32[]{:S(2)}, u32[]{:S(2)}) %collective-permute-start.24) | collective-permute-done | bytes 1048608 | tf_op jit(solution)/shard_map/ppermute | solution.py:202
  387.8 1.1 collective-permute-start.18
  388.9 8.2 %shard_map.112.refs_4_ = f32[128,128,512]{2,1,0:T(8,128)} custom-call(f32[128,128,512]{2,1,0:T(8,128)} %latent_ref.15, bf16[512,512]{1,0:T(8,128)(2,1)S(1)} %bitcast.55, bf16[32,128,128]{2,1,0:T(8,128)(2,1)S(1)} %get-tuple-element.95.refs_0_, bf16[32,128,128]{2,1,0:T(8,128)(2,1)S(1)} %collective-permute-done.25.refs_1_, ...), custom_call_target="tpu_custom_call" | custom-call | flops 134217728 | bytes 1310720 | tf_op jit(solution)/shard_map/pallas_call | solution.py:360
  397.1 8.2 %shard_map.113.refs_4_ = f32[128,128,512]{2,1,0:T(8,128)} custom-call(f32[128,128,512]{2,1,0:T(8,128)} %latent_ref.15, bf16[512,512]{1,0:T(8,128)(2,1)S(1)} %bitcast.56, bf16[32,128,128]{2,1,0:T(8,128)(2,1)S(1)} %get-tuple-element.91.refs_0_, bf16[32,128,128]{2,1,0:T(8,128)(2,1)S(1)} %collective-permute-done.22.refs_1_, ...), custom_call_target="tpu_custom_call", output_to_operand_aliasing={{}: (6, {})} | custom-call | flops 134217728 | bytes 1310720 | tf_op jit(solution)/shard_map/pallas_call | solution.py:360
  405.2 4.9 %collective-permute-done.20.refs_2_ = bf16[32,128,128]{2,1,0:T(8,128)(2,1)} collective-permute-done((bf16[32,128,128]{2,1,0:T(8,128)(2,1)}, bf16[32,128,128]{2,1,0:T(8,128)(2,1)}, u32[]{:S(2)}, u32[]{:S(2)}) %collective-permute-start.20) | collective-permute-done | bytes 1048608 | tf_op jit(solution)/shard_map/ppermute | solution.py:202
  410.2 21.7 %collective-permute-done.21.refs_3_ = bf16[32,128,128]{2,1,0:T(8,128)(2,1)} collective-permute-done((bf16[32,128,128]{2,1,0:T(8,128)(2,1)}, bf16[32,128,128]{2,1,0:T(8,128)(2,1)}, u32[]{:S(2)}, u32[]{:S(2)}) %collective-permute-start.21) | collective-permute-done | bytes 1048608 | tf_op jit(solution)/shard_map/ppermute | solution.py:202
  431.9 8.5 %shard_map.114.refs_4_ = f32[128,128,512]{2,1,0:T(8,128)} custom-call(f32[128,128,512]{2,1,0:T(8,128)} %latent_ref.15, bf16[512,512]{1,0:T(8,128)(2,1)S(1)} %bitcast.57, bf16[32,128,128]{2,1,0:T(8,128)(2,1)S(1)} %get-tuple-element.87.refs_0_, bf16[32,128,128]{2,1,0:T(8,128)(2,1)S(1)} %collective-permute-done.19.refs_1_, ...), custom_call_target="tpu_custom_call", output_to_operand_aliasing={{}: (6, {})} | custom-call | flops 134217728 | bytes 1310720 | tf_op jit(solution)/shard_map/pallas_call | solution.py:360
  440.4 1.0 copy-done.4
  441.4 13.7 %collective-permute-done.17.refs_2_ = bf16[32,128,128]{2,1,0:T(8,128)(2,1)} collective-permute-done((bf16[32,128,128]{2,1,0:T(8,128)(2,1)}, bf16[32,128,128]{2,1,0:T(8,128)(2,1)}, u32[]{:S(2)}, u32[]{:S(2)}) %collective-permute-start.17) | collective-permute-done | bytes 1048608 | tf_op jit(solution)/shard_map/ppermute | solution.py:202
  455.1 21.7 %collective-permute-done.18.refs_3_ = bf16[32,128,128]{2,1,0:T(8,128)(2,1)} collective-permute-done((bf16[32,128,128]{2,1,0:T(8,128)(2,1)}, bf16[32,128,128]{2,1,0:T(8,128)(2,1)}, u32[]{:S(2)}, u32[]{:S(2)}) %collective-permute-start.18) | collective-permute-done | bytes 1048608 | tf_op jit(solution)/shard_map/ppermute | solution.py:202
  476.8 1.2 copy-done.5
  478.1 8.5 %shard_map.115 = f32[128,128,512]{2,1,0:T(8,128)} custom-call(f32[128,128,512]{2,1,0:T(8,128)} %latent_ref.15, bf16[512,512]{1,0:T(8,128)(2,1)S(1)} %bitcast.58, bf16[32,128,128]{2,1,0:T(8,128)(2,1)S(1)} %copy-done.3, bf16[32,128,128]{2,1,0:T(8,128)(2,1)S(1)} %copy-done.5, ...), custom_call_target="tpu_custom_call", output_to_operand_aliasing={{}: (6, {})} | custom-call | flops 134217728 | bytes 1310720 | tf_op jit(solution)/shard_map/pallas_call | solution.py:360
  (84 shorter events, 13.6 us)
Async XLA Ops:
  0.0 10.6 %copy-start = (bf16[512,512]{1,0:T(8,128)(2,1)S(1)}, bf16[512,512]{1,0:T(8,128)(2,1)}, u32[]{:S(2)}) copy-start(bf16[512,512]{1,0:T(8,128)(2,1)} %param.12) | copy-start | bytes 1572868
  3.2 13.9 %all-to-all-start = ((f32[1,16,3,128]{3,0,2,1:T(1,128)}), f32[1,16,3,128]{3,0,2,1:T(1,128)S(1)}, u32[]{:S(2)}, u32[]{:S(2)}) async-start(f32[1,16,3,128]{3,0,2,1:T(1,128)} %pad_maximum_fusion), calls=%async_computation | async-start | bytes 49152 | tf_op jit(solution)/shard_map/all_to_all | solution.py:254
  23.6 15.9 %collective-permute-start.6 = (bf16[32,128,128]{2,1,0:T(8,128)(2,1)S(1)}, bf16[32,128,128]{2,1,0:T(8,128)(2,1)S(1)}, u32[]{:S(2)}, u32[]{:S(2)}) collective-permute-start(bf16[32,128,128]{2,1,0:T(8,128)(2,1)S(1)} %get-tuple-element.64), channel_id=1, source_target_pairs={{0,4},{4,0},{8,12},{12,8},{1,5},{5,1},{9,13},{13,9},{2,6},{6,2},{1... | collective-permute-start | bytes 3145736 | tf_op jit(solution)/shard_map/ppermute | solution.py:202
  29.4 1.0 copy-start.8
  30.4 9.8 %collective-permute-start.3 = (bf16[32,128,128]{2,1,0:T(8,128)(2,1)S(1)}, bf16[32,128,128]{2,1,0:T(8,128)(2,1)S(1)}, u32[]{:S(2)}, u32[]{:S(2)}) collective-permute-start(bf16[32,128,128]{2,1,0:T(8,128)(2,1)S(1)} %get-tuple-element.58), channel_id=1, source_target_pairs={{0,4},{4,0},{8,12},{12,8},{1,5},{5,1},{9,13},{13,9},{2,6},{6,2},{1... | collective-permute-start | bytes 3145736 | tf_op jit(solution)/shard_map/ppermute | solution.py:202
  30.8 26.0 %collective-permute-start.4 = (bf16[32,128,128]{2,1,0:T(8,128)(2,1)S(1)}, bf16[32,128,128]{2,1,0:T(8,128)(2,1)S(1)}, u32[]{:S(2)}, u32[]{:S(2)}) collective-permute-start(bf16[32,128,128]{2,1,0:T(8,128)(2,1)S(1)} %get-tuple-element.59), channel_id=1, source_target_pairs={{0,8},{4,12},{8,0},{12,4},{1,9},{5,13},{9,1},{13,5},{2,10},{6,14},... | collective-permute-start | bytes 3145736 | tf_op jit(solution)/shard_map/ppermute | solution.py:202
  31.4 46.3 %collective-permute-start.5 = (bf16[32,128,128]{2,1,0:T(8,128)(2,1)S(1)}, bf16[32,128,128]{2,1,0:T(8,128)(2,1)}, u32[]{:S(2)}, u32[]{:S(2)}) collective-permute-start(bf16[32,128,128]{2,1,0:T(8,128)(2,1)S(1)} %get-tuple-element.60), channel_id=1, source_target_pairs={{0,12},{4,8},{8,4},{12,0},{1,13},{5,9},{9,5},{13,1},{2,14},{6,10},... | collective-permute-start | bytes 3145736 | tf_op jit(solution)/shard_map/ppermute | solution.py:202
  37.8 1.0 copy-start.16
  38.8 48.4 %collective-permute-start = (bf16[32,128,128]{2,1,0:T(8,128)(2,1)S(1)}, bf16[32,128,128]{2,1,0:T(8,128)(2,1)S(1)}, u32[]{:S(2)}, u32[]{:S(2)}) collective-permute-start(bf16[32,128,128]{2,1,0:T(8,128)(2,1)S(1)} %get-tuple-element.53), channel_id=1, source_target_pairs={{0,4},{4,0},{8,12},{12,8},{1,5},{5,1},{9,13},{13,9},{2,6},{6,2},{1... | collective-permute-start | bytes 3145736 | tf_op jit(solution)/shard_map/ppermute | solution.py:202
  39.5 46.7 %copy-start.6 = (bf16[32,128,128]{2,1,0:T(8,128)(2,1)}, bf16[32,128,128]{2,1,0:T(8,128)(2,1)S(1)}, u32[]{:S(2)}) copy-start(bf16[32,128,128]{2,1,0:T(8,128)(2,1)S(1)} %collective-permute-done.6.refs_1_) | copy-start | bytes 3145732
  39.5 62.2 %collective-permute-start.1 = (bf16[32,128,128]{2,1,0:T(8,128)(2,1)S(1)}, bf16[32,128,128]{2,1,0:T(8,128)(2,1)S(1)}, u32[]{:S(2)}, u32[]{:S(2)}) collective-permute-start(bf16[32,128,128]{2,1,0:T(8,128)(2,1)S(1)} %get-tuple-element.54), channel_id=1, source_target_pairs={{0,8},{4,12},{8,0},{12,4},{1,9},{5,13},{9,1},{13,5},{2,10},{6,14},... | collective-permute-start | bytes 3145736 | tf_op jit(solution)/shard_map/ppermute | solution.py:202
  40.1 46.1 %copy-start.10 = (bf16[32,128,128]{2,1,0:T(8,128)(2,1)}, bf16[32,128,128]{2,1,0:T(8,128)(2,1)S(1)}, u32[]{:S(2)}) copy-start(bf16[32,128,128]{2,1,0:T(8,128)(2,1)S(1)} %collective-permute-done.3.refs_1_) | copy-start | bytes 3145732
  40.1 82.5 %collective-permute-start.2 = (bf16[32,128,128]{2,1,0:T(8,128)(2,1)S(1)}, bf16[32,128,128]{2,1,0:T(8,128)(2,1)}, u32[]{:S(2)}, u32[]{:S(2)}) collective-permute-start(bf16[32,128,128]{2,1,0:T(8,128)(2,1)S(1)} %get-tuple-element.55), channel_id=1, source_target_pairs={{0,12},{4,8},{8,4},{12,0},{1,13},{5,9},{9,5},{13,1},{2,14},{6,10},... | collective-permute-start | bytes 3145736 | tf_op jit(solution)/shard_map/ppermute | solution.py:202
  56.8 29.5 %copy-start.12 = (bf16[32,128,128]{2,1,0:T(8,128)(2,1)}, bf16[32,128,128]{2,1,0:T(8,128)(2,1)S(1)}, u32[]{:S(2)}) copy-start(bf16[32,128,128]{2,1,0:T(8,128)(2,1)S(1)} %collective-permute-done.4.refs_2_) | copy-start | bytes 3145732
  56.8 92.7 %collective-permute-start.7 = (bf16[32,128,128]{2,1,0:T(8,128)(2,1)}, bf16[32,128,128]{2,1,0:T(8,128)(2,1)}, u32[]{:S(2)}, u32[]{:S(2)}) collective-permute-start(bf16[32,128,128]{2,1,0:T(8,128)(2,1)} %get-tuple-element.65), channel_id=1, source_target_pairs={{0,8},{4,12},{8,0},{12,4},{1,9},{5,13},{9,1},{13,5},{2,10},{6,14},... | collective-permute-start | bytes 3145736 | tf_op jit(solution)/shard_map/ppermute | solution.py:202
  77.7 46.7 %copy-start.22 = (bf16[512,512]{1,0:T(8,128)(2,1)S(1)}, bf16[512,512]{1,0:T(8,128)(2,1)}, u32[]{:S(2)}) copy-start(bf16[512,512]{1,0:T(8,128)(2,1)} %param.11) | copy-start | bytes 1572868
  77.7 48.3 %copy-start.23 = (f32[128]{0:T(128)S(1)}, f32[128]{0:T(128)}, u32[]{:S(2)}) copy-start(f32[128]{0:T(128)} %param.13) | copy-start | bytes 1540
  77.7 89.9 %collective-permute-start.8 = (bf16[32,128,128]{2,1,0:T(8,128)(2,1)}, bf16[32,128,128]{2,1,0:T(8,128)(2,1)}, u32[]{:S(2)}, u32[]{:S(2)}) collective-permute-start(bf16[32,128,128]{2,1,0:T(8,128)(2,1)} %get-tuple-element.66), channel_id=1, source_target_pairs={{0,12},{4,8},{8,4},{12,0},{1,13},{5,9},{9,5},{13,1},{2,14},{6,10},... | collective-permute-start | bytes 3145736 | tf_op jit(solution)/shard_map/ppermute | solution.py:202
  86.2 1.0 copy-start.14
  87.2 1.0 copy-start.18
  88.2 87.6 %collective-permute-start.9 = (bf16[32,128,128]{2,1,0:T(8,128)(2,1)}, bf16[32,128,128]{2,1,0:T(8,128)(2,1)}, u32[]{:S(2)}, u32[]{:S(2)}) collective-permute-start(bf16[32,128,128]{2,1,0:T(8,128)(2,1)} %get-tuple-element.70), channel_id=1, source_target_pairs={{0,4},{4,0},{8,12},{12,8},{1,5},{5,1},{9,13},{13,9},{2,6},{6,2},{1... | collective-permute-start | bytes 3145736 | tf_op jit(solution)/shard_map/ppermute | solution.py:202
  101.7 1.0 copy-start.20
  102.7 89.0 %collective-permute-start.10 = (bf16[32,128,128]{2,1,0:T(8,128)(2,1)}, bf16[32,128,128]{2,1,0:T(8,128)(2,1)}, u32[]{:S(2)}, u32[]{:S(2)}) collective-permute-start(bf16[32,128,128]{2,1,0:T(8,128)(2,1)} %get-tuple-element.71), channel_id=1, source_target_pairs={{0,8},{4,12},{8,0},{12,4},{1,9},{5,13},{9,1},{13,5},{2,10},{6,14},... | collective-permute-start | bytes 3145736 | tf_op jit(solution)/shard_map/ppermute | solution.py:202
  122.6 89.9 %collective-permute-start.11 = (bf16[32,128,128]{2,1,0:T(8,128)(2,1)}, bf16[32,128,128]{2,1,0:T(8,128)(2,1)}, u32[]{:S(2)}, u32[]{:S(2)}) collective-permute-start(bf16[32,128,128]{2,1,0:T(8,128)(2,1)} %get-tuple-element.72), channel_id=1, source_target_pairs={{0,12},{4,8},{8,4},{12,0},{1,13},{5,9},{9,5},{13,1},{2,14},{6,10},... | collective-permute-start | bytes 3145736 | tf_op jit(solution)/shard_map/ppermute | solution.py:202
  125.9 41.6 %copy-start.7 = (bf16[32,128,128]{2,1,0:T(8,128)(2,1)S(1)}, bf16[32,128,128]{2,1,0:T(8,128)(2,1)}, u32[]{:S(2)}) copy-start(bf16[32,128,128]{2,1,0:T(8,128)(2,1)} %copy-done.6) | copy-start | bytes 3145732
  126.1 1.3 copy-start.17
  127.4 1.2 copy-start.19
  128.7 1.2 copy-start.21
  137.8 1.2 copy-start.9
  139.0 1.2 copy-start.11
  140.2 1.2 copy-start.13
  141.4 71.1 %copy-start.15 = (bf16[32,128,128]{2,1,0:T(8,128)(2,1)S(1)}, bf16[32,128,128]{2,1,0:T(8,128)(2,1)}, u32[]{:S(2)}) copy-start(bf16[32,128,128]{2,1,0:T(8,128)(2,1)} %copy-done.14) | copy-start | bytes 3145732
  220.9 8.8 %collective-permute-start.12 = (f32[512,128]{1,0:T(8,128)S(1)}, f32[512,128]{1,0:T(8,128)S(1)}, u32[]{:S(2)}, u32[]{:S(2)}) collective-permute-start(f32[512,128]{1,0:T(8,128)S(1)} %get-tuple-element.78), channel_id=1, source_target_pairs={{0,1},{1,2},{2,3},{4,5},{5,6},{6,7},{8,9},{9,10},{10,11},{12,13},{... | collective-permute-start | bytes 786440 | tf_op jit(solution)/shard_map/ppermute | solution.py:211
  229.7 10.1 %collective-permute-start.13 = (f32[512,128]{1,0:T(8,128)S(1)}, f32[512,128]{1,0:T(8,128)S(1)}, u32[]{:S(2)}, u32[]{:S(2)}) collective-permute-start(f32[512,128]{1,0:T(8,128)S(1)} %add.103), channel_id=1, source_target_pairs={{0,2},{1,3},{4,6},{5,7},{8,10},{9,11},{12,14},{13,15},{16,18},{17,... | collective-permute-start | bytes 786440 | tf_op jit(solution)/shard_map/ppermute | solution.py:211
  247.7 13.7 %collective-permute-start.14 = (f32[512,128]{1,0:T(8,128)S(1)}, f32[512,128]{1,0:T(8,128)S(1)}, u32[]{:S(2)}, u32[]{:S(2)}) collective-permute-start(f32[512,128]{1,0:T(8,128)S(1)} %fusion), channel_id=1, source_target_pairs={{1,0},{2,1},{3,2},{5,4},{6,5},{7,6},{9,8},{10,9},{11,10},{13,12},{... | collective-permute-start | bytes 786440 | tf_op jit(solution)/shard_map/ppermute | solution.py:211
  261.4 15.1 %collective-permute-start.15 = (f32[512,128]{1,0:T(8,128)S(1)}, f32[512,128]{1,0:T(8,128)S(1)}, u32[]{:S(2)}, u32[]{:S(2)}) collective-permute-start(f32[512,128]{1,0:T(8,128)S(1)} %add.106), channel_id=1, source_target_pairs={{2,0},{3,1},{6,4},{7,5},{10,8},{11,9},{14,12},{15,13},{18,16},{19,... | collective-permute-start | bytes 786440 | tf_op jit(solution)/shard_map/ppermute | solution.py:211
  294.2 34.3 %collective-permute-start.25 = (bf16[32,128,128]{2,1,0:T(8,128)(2,1)}, bf16[32,128,128]{2,1,0:T(8,128)(2,1)S(1)}, u32[]{:S(2)}, u32[]{:S(2)}) collective-permute-start(bf16[32,128,128]{2,1,0:T(8,128)(2,1)} %get-tuple-element.96), channel_id=1, source_target_pairs={{0,4},{4,0},{8,12},{12,8},{1,5},{5,1},{9,13},{13,9},{2,6},{6,2},{1... | collective-permute-start | bytes 3145736 | tf_op jit(solution)/shard_map/ppermute | solution.py:202
  294.2 35.1 %collective-permute-start.26 = (bf16[32,128,128]{2,1,0:T(8,128)(2,1)S(1)}, bf16[32,128,128]{2,1,0:T(8,128)(2,1)S(1)}, u32[]{:S(2)}, u32[]{:S(2)}) collective-permute-start(bf16[32,128,128]{2,1,0:T(8,128)(2,1)S(1)} %get-tuple-element.97), channel_id=1, source_target_pairs={{0,8},{4,12},{8,0},{12,4},{1,9},{5,13},{9,1},{13,5},{2,10},{6,14},... | collective-permute-start | bytes 3145736 | tf_op jit(solution)/shard_map/ppermute | solution.py:202
  295.1 46.8 %collective-permute-start.27 = (bf16[32,128,128]{2,1,0:T(8,128)(2,1)S(1)}, bf16[32,128,128]{2,1,0:T(8,128)(2,1)S(1)}, u32[]{:S(2)}, u32[]{:S(2)}) collective-permute-start(bf16[32,128,128]{2,1,0:T(8,128)(2,1)S(1)} %get-tuple-element.98), channel_id=1, source_target_pairs={{0,12},{4,8},{8,4},{12,0},{1,13},{5,9},{9,5},{13,1},{2,14},{6,10},... | collective-permute-start | bytes 3145736 | tf_op jit(solution)/shard_map/ppermute | solution.py:202
  311.8 31.0 %collective-permute-start.22 = (bf16[32,128,128]{2,1,0:T(8,128)(2,1)}, bf16[32,128,128]{2,1,0:T(8,128)(2,1)S(1)}, u32[]{:S(2)}, u32[]{:S(2)}) collective-permute-start(bf16[32,128,128]{2,1,0:T(8,128)(2,1)} %get-tuple-element.92), channel_id=1, source_target_pairs={{0,4},{4,0},{8,12},{12,8},{1,5},{5,1},{9,13},{13,9},{2,6},{6,2},{1... | collective-permute-start | bytes 3145736 | tf_op jit(solution)/shard_map/ppermute | solution.py:202
  312.2 52.9 %collective-permute-start.23 = (bf16[32,128,128]{2,1,0:T(8,128)(2,1)}, bf16[32,128,128]{2,1,0:T(8,128)(2,1)S(1)}, u32[]{:S(2)}, u32[]{:S(2)}) collective-permute-start(bf16[32,128,128]{2,1,0:T(8,128)(2,1)} %get-tuple-element.93), channel_id=1, source_target_pairs={{0,8},{4,12},{8,0},{12,4},{1,9},{5,13},{9,1},{13,5},{2,10},{6,14},... | collective-permute-start | bytes 3145736 | tf_op jit(solution)/shard_map/ppermute | solution.py:202
  328.6 58.4 %collective-permute-start.24 = (bf16[32,128,128]{2,1,0:T(8,128)(2,1)}, bf16[32,128,128]{2,1,0:T(8,128)(2,1)}, u32[]{:S(2)}, u32[]{:S(2)}) collective-permute-start(bf16[32,128,128]{2,1,0:T(8,128)(2,1)} %get-tuple-element.94), channel_id=1, source_target_pairs={{0,12},{4,8},{8,4},{12,0},{1,13},{5,9},{9,5},{13,1},{2,14},{6,10},... | collective-permute-start | bytes 3145736 | tf_op jit(solution)/shard_map/ppermute | solution.py:202
  329.4 58.4 %collective-permute-start.19 = (bf16[32,128,128]{2,1,0:T(8,128)(2,1)}, bf16[32,128,128]{2,1,0:T(8,128)(2,1)S(1)}, u32[]{:S(2)}, u32[]{:S(2)}) collective-permute-start(bf16[32,128,128]{2,1,0:T(8,128)(2,1)} %get-tuple-element.88), channel_id=1, source_target_pairs={{0,4},{4,0},{8,12},{12,8},{1,5},{5,1},{9,13},{13,9},{2,6},{6,2},{1... | collective-permute-start | bytes 3145736 | tf_op jit(solution)/shard_map/ppermute | solution.py:202
  341.9 68.3 %collective-permute-start.20 = (bf16[32,128,128]{2,1,0:T(8,128)(2,1)}, bf16[32,128,128]{2,1,0:T(8,128)(2,1)}, u32[]{:S(2)}, u32[]{:S(2)}) collective-permute-start(bf16[32,128,128]{2,1,0:T(8,128)(2,1)} %get-tuple-element.89), channel_id=1, source_target_pairs={{0,8},{4,12},{8,0},{12,4},{1,9},{5,13},{9,1},{13,5},{2,10},{6,14},... | collective-permute-start | bytes 3145736 | tf_op jit(solution)/shard_map/ppermute | solution.py:202
  342.8 89.1 %collective-permute-start.21 = (bf16[32,128,128]{2,1,0:T(8,128)(2,1)}, bf16[32,128,128]{2,1,0:T(8,128)(2,1)}, u32[]{:S(2)}, u32[]{:S(2)}) collective-permute-start(bf16[32,128,128]{2,1,0:T(8,128)(2,1)} %get-tuple-element.90), channel_id=1, source_target_pairs={{0,12},{4,8},{8,4},{12,0},{1,13},{5,9},{9,5},{13,1},{2,14},{6,10},... | collective-permute-start | bytes 3145736 | tf_op jit(solution)/shard_map/ppermute | solution.py:202
  361.8 35.2 %copy-start.2 = (bf16[32,128,128]{2,1,0:T(8,128)(2,1)}, bf16[32,128,128]{2,1,0:T(8,128)(2,1)S(1)}, u32[]{:S(2)}) copy-start(bf16[32,128,128]{2,1,0:T(8,128)(2,1)S(1)} %get-tuple-element.83.refs_0_) | copy-start | bytes 3145732
  365.1 75.2 %collective-permute-start.16 = (bf16[32,128,128]{2,1,0:T(8,128)(2,1)}, bf16[32,128,128]{2,1,0:T(8,128)(2,1)S(1)}, u32[]{:S(2)}, u32[]{:S(2)}) collective-permute-start(bf16[32,128,128]{2,1,0:T(8,128)(2,1)} %get-tuple-element.84), channel_id=1, source_target_pairs={{0,4},{4,0},{8,12},{12,8},{1,5},{5,1},{9,13},{13,9},{2,6},{6,2},{1... | collective-permute-start | bytes 3145736 | tf_op jit(solution)/shard_map/ppermute | solution.py:202
  386.9 68.2 %collective-permute-start.17 = (bf16[32,128,128]{2,1,0:T(8,128)(2,1)}, bf16[32,128,128]{2,1,0:T(8,128)(2,1)}, u32[]{:S(2)}, u32[]{:S(2)}) collective-permute-start(bf16[32,128,128]{2,1,0:T(8,128)(2,1)} %get-tuple-element.85), channel_id=1, source_target_pairs={{0,8},{4,12},{8,0},{12,4},{1,9},{5,13},{9,1},{13,5},{2,10},{6,14},... | collective-permute-start | bytes 3145736 | tf_op jit(solution)/shard_map/ppermute | solution.py:202
  387.8 89.0 %collective-permute-start.18 = (bf16[32,128,128]{2,1,0:T(8,128)(2,1)}, bf16[32,128,128]{2,1,0:T(8,128)(2,1)}, u32[]{:S(2)}, u32[]{:S(2)}) collective-permute-start(bf16[32,128,128]{2,1,0:T(8,128)(2,1)} %get-tuple-element.86), channel_id=1, source_target_pairs={{0,12},{4,8},{8,4},{12,0},{1,13},{5,9},{9,5},{13,1},{2,14},{6,10},... | collective-permute-start | bytes 3145736 | tf_op jit(solution)/shard_map/ppermute | solution.py:202
  431.9 44.9 %copy-start.3 = (bf16[32,128,128]{2,1,0:T(8,128)(2,1)S(1)}, bf16[32,128,128]{2,1,0:T(8,128)(2,1)}, u32[]{:S(2)}) copy-start(bf16[32,128,128]{2,1,0:T(8,128)(2,1)} %copy-done.2) | copy-start | bytes 3145732
  440.4 1.0 copy-start.4
  476.8 1.2 copy-start.5
  478.1 8.5 %copy-start.1 = (bf16[512,512]{1,0:T(8,128)(2,1)S(1)}, bf16[512,512]{1,0:T(8,128)(2,1)}, u32[]{:S(2)}) copy-start(bf16[512,512]{1,0:T(8,128)(2,1)} %param.12) | copy-start | bytes 1572868
